TPU v7x, 32 devices: a whole 2x2x4 slice. The times are simulated.
32 devices in a mesh: group: 4 (over y, x), local: 8 (over z, core).
Axes of the slice: x: 2, y: 2, z: 4, core: 2. Of those that a mesh axis runs over, the one named last changes fastest.
Arguments:
- features: bfloat16 [192, 7168], P(('group', 'local')), may hold values from -6 to 6
- cotangent: bfloat16 [192, 7168], P(('group', 'local')), may hold values from -6 to 6
- expert_ids: int32 [192, 4], P(('group', 'local')), may hold values from 0 to 7, as said below
- gates: float32 [192, 4], P(('group', 'local')), may hold values from 0.1 to 1
- w_gate: bfloat16 [8, 7168, 2048], P('local', None, 'group'), may hold values from -0.0625 to 0.0625
- w_up: bfloat16 [8, 7168, 2048], P('local', None, 'group'), may hold values from -0.0625 to 0.0625
- w_down: bfloat16 [8, 2048, 7168], P('local', 'group'), may hold values from -0.125 to 0.125
Outputs:
- grad_features: float32 [192, 7168], P(('group', 'local'))
- grad_gate: bfloat16 [8, 7168, 2048], P('local', None, 'group')
- grad_up: bfloat16 [8, 7168, 2048], P('local', None, 'group')
- grad_down: bfloat16 [8, 2048, 7168], P('local', 'group')
Inputs may be any that keep to these rules, and one draw needn't show every extreme that they name: `expert_ids`: each row names 4 different experts, all of them in at most 3 expert groups, expert e lying in group e // 2.
All inputs are finite; a program needn't handle non-finite values.
Results may differ from a plain program's by a relative error of at most 0.013.
Values may be sent and summed in bfloat16 or wider, within the bound.
A program may use at most 192 MiB of HBM per device.

v0:
```python
import jax
import jax.numpy as jnp
from jax import lax
from jax.sharding import PartitionSpec as P


def silu_parts(pre):
    sig = jax.nn.sigmoid(pre)
    return (pre * sig, sig * (1.0 + pre * (1.0 - sig)))


def body(features, cotangent, expert_ids, gates, w_gate, w_up, w_down):
    experts = lax.axis_size("local")
    groups = lax.axis_size("group")
    tok_rows = features.shape[0]
    width = features.shape[1]
    choices_per = expert_ids.shape[1]
    slot_count = max(2, 2 * tok_rows * choices_per // experts)
    hits = (expert_ids[..., None] == jnp.arange(experts, dtype=jnp.int32)).astype(jnp.int32)
    counts = jnp.sum(hits, axis=1)
    before = jnp.cumsum(counts, axis=0) - counts
    slots = jnp.sum(hits * before[:, None, :], axis=2)
    code = jnp.where(slots < slot_count, expert_ids * slot_count + slots, -1)
    match = code[None, :, :] == jnp.arange(experts * slot_count, dtype=jnp.int32)[:, None, None]
    pick = jnp.sum(match.astype(jnp.float32), axis=2)
    scale = jnp.sum(jnp.where(match, gates[None, :, :], 0.0), axis=2)
    x_bins = jnp.dot(pick.astype(jnp.bfloat16), features, preferred_element_type=jnp.float32)
    x_bins = x_bins.astype(jnp.bfloat16).reshape(experts, slot_count, width)
    g_bins = jnp.dot(scale, cotangent.astype(jnp.float32), precision=lax.Precision.HIGHEST)
    g_bins = g_bins.astype(jnp.bfloat16).reshape(experts, slot_count, width)
    first = (
        lax.all_to_all(x_bins, "local", split_axis=0, concat_axis=0, tiled=True),
        lax.all_to_all(g_bins, "local", split_axis=0, concat_axis=0, tiled=True),
    )
    arrived = (
        lax.all_gather(first[0][None], "group", axis=0, tiled=True),
        lax.all_gather(first[1][None], "group", axis=0, tiled=True),
    )
    total_rows = groups * experts * slot_count
    rows_x = arrived[0].reshape(total_rows, width)
    rows_g = arrived[1].reshape(total_rows, width)
    gate_w = w_gate[0]
    up_w = w_up[0]
    down_w = w_down[0]
    pre_gate = jnp.dot(rows_x, gate_w, preferred_element_type=jnp.float32)
    pre_up = jnp.dot(rows_x, up_w, preferred_element_type=jnp.float32)
    act, slope = silu_parts(pre_gate)
    hidden = (act * pre_up).astype(jnp.bfloat16)
    grad_down = jnp.dot(hidden.T, rows_g, preferred_element_type=jnp.float32).astype(jnp.bfloat16)
    d_hidden = jnp.dot(rows_g, down_w.T, preferred_element_type=jnp.float32)
    d_gate = (d_hidden * pre_up * slope).astype(jnp.bfloat16)
    d_up = (d_hidden * act).astype(jnp.bfloat16)
    grad_gate = jnp.dot(rows_x.T, d_gate, preferred_element_type=jnp.float32).astype(jnp.bfloat16)
    grad_up = jnp.dot(rows_x.T, d_up, preferred_element_type=jnp.float32).astype(jnp.bfloat16)
    partial_value = jnp.dot(d_gate, gate_w.T, preferred_element_type=jnp.float32)
    partial_value = partial_value + jnp.dot(d_up, up_w.T, preferred_element_type=jnp.float32)
    partial_value = lax.optimization_barrier(partial_value.astype(jnp.bfloat16))
    summed_here = lax.psum_scatter(
        partial_value.astype(jnp.float32)
        .reshape(groups, experts, slot_count, width)
        .astype(jnp.bfloat16),
        "group",
        scatter_dimension=0,
        tiled=True,
    ).astype(jnp.float32)
    summed = lax.all_to_all(
        summed_here[0].astype(jnp.bfloat16), "local", split_axis=0, concat_axis=0, tiled=True
    ).astype(jnp.float32)
    bin_dx = summed.reshape(experts * slot_count, width)
    grad_features = jnp.dot(pick.T, bin_dx, precision=lax.Precision.HIGHEST)
    return (grad_features, grad_gate[None], grad_up[None], grad_down[None])


def solution(mesh):
    in_specs = (
        P(("group", "local"), None),
        P(("group", "local"), None),
        P(("group", "local"), None),
        P(("group", "local"), None),
        P("local", None, "group"),
        P("local", None, "group"),
        P("local", "group", None),
    )
    out_specs = (
        P(("group", "local"), None),
        P("local", None, "group"),
        P("local", None, "group"),
        P("local", "group", None),
    )
    return jax.shard_map(body, mesh=mesh, in_specs=in_specs, out_specs=out_specs, check_vma=False)
```

profile of v0, /device:TPU:0, one launch (start us, length us, event | category | flops | bytes accessed | tf_op | source)
XLA Modules:
  0.0 241.0 jit_solution(16829746015942513762)
XLA Ops:
  7.2 0.0 copy-start
  7.2 0.0 copy-start.5
  7.2 0.0 all-gather.7.cloned.1.call-start
  7.2 0.8 copy.35
  8.1 0.1 convert_reduce_fusion.1
  8.2 0.2 select_reduce_fusion.1
  8.4 0.8 copy.37
  9.2 0.1 select_reduce_fusion
  9.3 0.0 copy-done
  9.3 0.4 convolution_convert_fusion.3
  9.7 0.2 reshape.40
  10.0 29.9 %all_to_all.15 = bf16[8,6,7168]{2,1,0:T(8,128)(2,1)S(1)} all-to-all(bf16[8,6,7168]{2,1,0:T(8,128)(2,1)S(1)} %reshape.40), channel_id=1, replica_groups=mesh['group'=4,'local'=8] {'local'}, dimensions={0} | all-to-all | bytes 1376256 | tf_op jit(solution)/shard_map/all_to_all | solution.py:32
  39.9 1.2 copy.40
  41.1 0.0 all-gather.7.cloned.1.call-update
  41.1 0.0 all-gather.5.cloned.1.call-start
  41.2 0.0 copy-done.5
  41.2 0.8 convolution_convert_fusion.4
  42.0 0.2 reshape.38
  42.2 26.2 %all_to_all.16 = bf16[8,6,7168]{2,1,0:T(8,128)(2,1)S(1)} all-to-all(bf16[8,6,7168]{2,1,0:T(8,128)(2,1)S(1)} %reshape.38), channel_id=1, replica_groups=mesh['group'=4,'local'=8] {'local'}, dimensions={0} | all-to-all | bytes 1376256 | tf_op jit(solution)/shard_map/all_to_all | solution.py:33
  68.4 1.2 copy.38
  69.6 0.0 all-gather.5.cloned.1.call-update
  69.7 0.0 reduce-scatter.4.cloned.1.call-start
  69.7 11.2 %all-gather.7.cloned.1.call-done = bf16[32,6,7168]{2,0,1:T(8,128)(2,1)} async-done(((bf16[8,6,7168]{2,0,1:T(8,128)(2,1)}), bf16[32,6,7168]{2,0,1:T(8,128)(2,1)}) %all-gather.7.cloned.1.call-update) | async-done | bytes 2752528 | tf_op jit(solution)/shard_map/all_gather | solution.py:36
  80.9 5.2 %copy.41 = bf16[32,6,7168]{2,1,0:T(8,128)(2,1)} copy(bf16[32,6,7168]{2,0,1:T(8,128)(2,1)} %all-gather.7.cloned.1.call-done) | data formatting | bytes 5505024 | tf_op jit(solution)/shard_map/all_gather | solution.py:36
  86.1 3.2 %reshape.41 = bf16[192,7168]{1,0:T(8,128)(2,1)S(1)} reshape(bf16[32,6,7168]{2,1,0:T(8,128)(2,1)} %copy.41) | data formatting | bytes 5505024 | tf_op jit(solution)/shard_map/reshape | solution.py:40
  89.3 6.0 %fusion.6 = f32[192,512]{1,0:T(8,128)} fusion(bf16[192,7168]{1,0:T(8,128)(2,1)S(1)} %reshape.41, bf16[1,7168,512]{2,1,0:T(8,128)(2,1)} %param.11), kind=kOutput, calls=%fused_computation.12 | convolution fusion | flops 1409286144 | bytes 10485760 | tf_op jit(solution)/shard_map/dot_general | solution.py:45
  95.3 5.4 %fusion.9 = f32[192,512]{1,0:T(8,128)} fusion(bf16[192,7168]{1,0:T(8,128)(2,1)S(1)} %reshape.41, bf16[1,7168,512]{2,1,0:T(8,128)(2,1)} %param.12), kind=kOutput, calls=%fused_computation.15 | convolution fusion | flops 1409286144 | bytes 10485760 | tf_op jit(solution)/shard_map/dot_general | solution.py:46
  100.7 23.4 %all-gather.5.cloned.1.call-done = bf16[32,6,7168]{2,0,1:T(8,128)(2,1)} async-done(((bf16[8,6,7168]{2,0,1:T(8,128)(2,1)}), bf16[32,6,7168]{2,0,1:T(8,128)(2,1)}) %all-gather.5.cloned.1.call-update) | async-done | bytes 2752528 | tf_op jit(solution)/shard_map/all_gather | solution.py:37
  124.1 5.2 %copy.39 = bf16[32,6,7168]{2,1,0:T(8,128)(2,1)} copy(bf16[32,6,7168]{2,0,1:T(8,128)(2,1)} %all-gather.5.cloned.1.call-done) | data formatting | bytes 5505024 | tf_op jit(solution)/shard_map/all_gather | solution.py:37
  129.2 4.6 %reshape.39 = bf16[192,7168]{1,0:T(8,128)(2,1)} reshape(bf16[32,6,7168]{2,1,0:T(8,128)(2,1)} %copy.39) | data formatting | bytes 5505024 | tf_op jit(solution)/shard_map/reshape | solution.py:41
  133.9 6.8 %multiply_convert_fusion.1 = (bf16[192,512]{1,0:T(8,128)(2,1)S(1)}, bf16[192,512]{1,0:T(8,128)(2,1)S(1)}) fusion(f32[192,512]{1,0:T(8,128)} %fusion.6, f32[192,512]{1,0:T(8,128)} %fusion.9, bf16[192,7168]{1,0:T(8,128)(2,1)} %reshape.39, bf16[1,512,7168]{2,1,0:T(8,128)(2,1)} %param.13), kind=kOutput, calls=%fused_computation.20 | convolution fusion | flops 1410564096 | bytes 11272192 | tf_op jit(solution)/shard_map/dot_general | solution.py:50
  140.6 0.0 slice-start.1
  140.7 5.8 %fusion.4 = f32[192,7168]{1,0:T(8,128)S(1)} fusion(bf16[192,512]{1,0:T(8,128)(2,1)S(1)} %get-tuple-element.7, bf16[1,7168,512]{2,1,0:T(8,128)(2,1)} %param.11), kind=kOutput, calls=%fused_computation.10 | convolution fusion | flops 1409286144 | bytes 13041664 | tf_op jit(solution)/shard_map/dot_general | solution.py:55
  146.4 0.0 slice-done
  146.4 4.1 %fusion.3 = bf16[192,7168]{1,0:T(8,128)(2,1)} fusion(f32[192,7168]{1,0:T(8,128)S(1)} %fusion.4, bf16[192,512]{1,0:T(8,128)(2,1)S(1)} %get-tuple-element.6, bf16[1,7168,512]{2,1,0:T(8,128)(2,1)S(1)} %bitcast.39), kind=kOutput, calls=%fused_computation.7 | convolution fusion | flops 1412038656 | bytes 15794176 | tf_op jit(solution)/shard_map/dot_general | solution.py:56
  150.5 4.6 %convert_element_type.56 = bf16[4,8,6,7168]{3,2,1,0:T(8,128)(2,1)} reshape(bf16[192,7168]{1,0:T(8,128)(2,1)} %fusion.3) | data formatting | bytes 5505024 | tf_op jit(solution)/shard_map/convert_element_type | solution.py:61
  155.1 5.1 %copy.42 = bf16[4,8,6,7168]{3,1,2,0:T(8,128)(2,1)} copy(bf16[4,8,6,7168]{3,2,1,0:T(8,128)(2,1)} %convert_element_type.56) | data formatting | bytes 5505024 | tf_op jit(solution)/shard_map/convert_element_type | solution.py:61
  160.2 0.0 reduce-scatter.4.cloned.1.call-update
  160.2 40.8 %reduce-scatter.4.cloned.1.call-done = bf16[1,8,6,7168]{3,1,2,0:T(8,128)(2,1)} async-done(((bf16[4,8,6,7168]{3,1,2,0:T(8,128)(2,1)}), bf16[1,8,6,7168]{3,1,2,0:T(8,128)(2,1)}) %reduce-scatter.4.cloned.1.call-update) | async-done | bytes 688144
  201.0 2.4 %copy.43 = bf16[8,6,7168]{2,1,0:T(8,128)(2,1)} copy(bf16[8,6,7168]{2,0,1:T(8,128)(2,1)} %bitcast.40) | data formatting | bytes 1376256 | tf_op jit(solution)/shard_map/convert_element_type | solution.py:67
  203.4 4.6 %all-to-all-start.2 = ((bf16[8,6,7168]{2,1,0:T(8,128)(2,1)}), bf16[8,6,7168]{2,1,0:T(8,128)(2,1)}, u32[]{:S(2)}, u32[]{:S(2)}) async-start(bf16[8,6,7168]{2,1,0:T(8,128)(2,1)} %copy.43), calls=%async_computation.2 | async-start | bytes 1835008 | tf_op jit(solution)/shard_map/all_to_all | solution.py:66
  208.0 5.2 %fusion.1 = bf16[1,7168,512]{2,1,0:T(8,128)(2,1)} fusion(bf16[192,7168]{1,0:T(8,128)(2,1)S(1)} %reshape.41, bf16[192,512]{1,0:T(8,128)(2,1)S(1)} %get-tuple-element.6), kind=kOutput, calls=%fused_computation.4 | convolution fusion | flops 1412956160 | bytes 10289152 | tf_op jit(solution)/shard_map/dot_general | solution.py:54
  213.2 5.2 %fusion = bf16[1,7168,512]{2,1,0:T(8,128)(2,1)} fusion(bf16[192,7168]{1,0:T(8,128)(2,1)S(1)} %reshape.41, bf16[192,512]{1,0:T(8,128)(2,1)S(1)} %get-tuple-element.7), kind=kOutput, calls=%fused_computation.3 | convolution fusion | flops 1412956160 | bytes 10289152 | tf_op jit(solution)/shard_map/dot_general | solution.py:53
  218.4 0.0 copy-done.3
  218.4 5.2 %fusion.2 = bf16[1,512,7168]{2,1,0:T(8,128)(2,1)} fusion(bf16[192,7168]{1,0:T(8,128)(2,1)S(1)} %copy-done.2, f32[192,512]{1,0:T(8,128)S(1)} %copy-done.4, f32[192,512]{1,0:T(8,128)S(1)} %copy-done.3), kind=kOutput, calls=%fused_computation.5 | convolution fusion | flops 1413545984 | bytes 10878976 | tf_op jit(solution)/shard_map/dot_general | solution.py:49
  223.5 8.4 %all-to-all-done.2 = bf16[8,6,7168]{2,1,0:T(8,128)(2,1)} async-done(((bf16[8,6,7168]{2,1,0:T(8,128)(2,1)}), bf16[8,6,7168]{2,1,0:T(8,128)(2,1)}, u32[]{:S(2)}, u32[]{:S(2)}) %all-to-all-start.2) | async-done | bytes 688160 | tf_op jit(solution)/shard_map/all_to_all | solution.py:66
  231.9 1.4 reshape.42
  233.4 1.1 fusion.17
  (13 shorter events, 0.1 us)
Async XLA Ops:
  7.2 2.1 copy-start
  7.2 34.0 %copy-start.5 = (bf16[6,7168]{1,0:T(8,128)(2,1)S(1)}, bf16[6,7168]{1,0:T(8,128)(2,1)}, u32[]{:S(2)}) copy-start(bf16[6,7168]{1,0:T(8,128)(2,1)} %param.8) | copy-start | bytes 258052
  7.2 73.7 %all-gather.7.cloned.1.call-start = ((), (), s32[]{:S(2)}) async-start(), calls=%async_computation.5 | async-start | bytes 3440640 | tf_op jit(solution)/shard_map/all_gather | solution.py:36
  41.1 83.0 %all-gather.5.cloned.1.call-start = ((), (), s32[]{:S(2)}) async-start(), calls=%async_computation.4 | async-start | bytes 3440640 | tf_op jit(solution)/shard_map/all_gather | solution.py:37
  69.7 131.4 %reduce-scatter.4.cloned.1.call-start = ((), (), s32[]{:S(2)}) async-start(), calls=%async_computation.6 | async-start | bytes 3440640
  133.9 12.5 %slice-start = ((s8[7340032]{0:T(1024)(128)(4,1)}), s8[4194304]{0:T(1024)(128)(4,1)S(1)}, s32[]{:S(2)}) async-start(s8[7340032]{0:T(1024)(128)(4,1)} %bitcast.38), calls=%async_computation.7 | async-start | bytes 8388608
  140.6 5.8 %slice-start.1 = ((s8[7340032]{0:T(1024)(128)(4,1)}), s8[3145728]{0:T(1024)(128)(4,1)S(1)}, s32[]{:S(2)}) async-start(s8[7340032]{0:T(1024)(128)(4,1)} %bitcast.38), calls=%async_computation.8 | async-start | bytes 6291456
  203.4 28.5 %all-to-all-start.2 = ((bf16[8,6,7168]{2,1,0:T(8,128)(2,1)}), bf16[8,6,7168]{2,1,0:T(8,128)(2,1)}, u32[]{:S(2)}, u32[]{:S(2)}) async-start(bf16[8,6,7168]{2,1,0:T(8,128)(2,1)} %copy.43), calls=%async_computation.2 | async-start | bytes 1835008 | tf_op jit(solution)/shard_map/all_to_all | solution.py:66
  213.2 5.2 %copy-start.2 = (bf16[192,7168]{1,0:T(8,128)(2,1)S(1)}, bf16[192,7168]{1,0:T(8,128)(2,1)}, u32[]{:S(2)}) copy-start(bf16[192,7168]{1,0:T(8,128)(2,1)} %reshape.39) | copy-start | bytes 8257540
  213.2 5.2 %copy-start.3 = (f32[192,512]{1,0:T(8,128)S(1)}, f32[192,512]{1,0:T(8,128)}, u32[]{:S(2)}) copy-start(f32[192,512]{1,0:T(8,128)} %fusion.6) | copy-start | bytes 1179652
  213.2 5.2 %copy-start.4 = (f32[192,512]{1,0:T(8,128)S(1)}, f32[192,512]{1,0:T(8,128)}, u32[]{:S(2)}) copy-start(f32[192,512]{1,0:T(8,128)} %fusion.9) | copy-start | bytes 1179652
  213.2 21.2 %copy-start.1 = (bf16[6,7168]{1,0:T(8,128)(2,1)S(1)}, bf16[6,7168]{1,0:T(8,128)(2,1)}, u32[]{:S(2)}) copy-start(bf16[6,7168]{1,0:T(8,128)(2,1)} %param.7) | copy-start | bytes 258052
Sparse Core Ops, SparseCore 0:
  41.3 39.6 all-gather.6
  83.3 40.7 all-gather.4
  160.3 40.6 reduce-scatter.3
where the time goes:
time: 242 us; the launch traced here: 241 us
  waiting for transfers between devices  83.8 us (35%)
  blocking collectives  56.1 us (23%)
  matrix products  45.7 us (19%)
  local copies, waits for them, and re-layouts  36.2 us (15%)
  between operations  13.9 us (6%)
  starting transfers between devices  4.73 us (2%)
    unnamed x4, waiting for transfers between devices  40.9 us
    all_to_all x1, blocking collectives, body(): lax.all_to_all(x_bins, 'local', split_axis=0, concat_axis=0, tiled=True)  29.9 us
    all_to_all x1, blocking collectives, body(): lax.all_to_all(g_bins, 'local', split_axis=0, concat_axis=0, tiled=True)  26.2 us
    all_gather x1, waiting for transfers between devices, body(): lax.all_gather(first[1][None], 'group', axis=0, tiled=True)  23.4 us
    all_gather x1, waiting for transfers between devices, body(): lax.all_gather(first[0][None], 'group', axis=0, tiled=True)  11.2 us
    convert_element_type x2, local copies, waits for them, and re-layouts, body(): summed_here = lax.psum_scatter(partial_value.astype(jnp.float32).reshape(...  9.67 us
    all_to_all x1, waiting for transfers between devices, body(): lax.all_to_all(summed_here[0].astype(jnp.bfloat16), 'local', split_axis=0...  8.38 us
    dot_general x1, matrix products, body(): d_hidden = jnp.dot(rows_g, down_w.T, preferred_element_type=jnp.float32)  6.76 us
  transfers between devices with their start and end apart: 4, of which 4 were waited for; matrix products, arithmetic and copies ran while one was open for 16% of the time, Pallas kernels for 0%

commit v1 on v0

v1 whole, which is shorter than its diff:
```python
import jax
import jax.numpy as jnp
from jax import lax
from jax.sharding import PartitionSpec as P

BOTH = ("group", "local")


def silu_parts(pre):
    sig = jax.nn.sigmoid(pre)
    return (pre * sig, sig * (1.0 + pre * (1.0 - sig)))


def body(features, cotangent, expert_ids, gates, w_gate, w_up, w_down):
    experts = lax.axis_size("local")
    devices = experts * lax.axis_size("group")
    tok_rows, width = features.shape
    rows = devices * tok_rows
    hits = expert_ids[..., None] == jnp.arange(experts, dtype=jnp.int32)
    on = jnp.sum(hits.astype(jnp.float32), axis=1)
    weight = jnp.sum(jnp.where(hits, gates[..., None], 0.0), axis=1)
    routes = lax.all_gather(jnp.concatenate([on, weight], axis=1)[None], BOTH, axis=0, tiled=True)
    all_x = lax.all_gather(features[None], BOTH, axis=0, tiled=True)
    all_g = lax.all_gather(cotangent[None], BOTH, axis=0, tiled=True)
    me = lax.axis_index("local")
    routes = routes.reshape(rows, 2 * experts)
    on = lax.dynamic_slice_in_dim(routes, me, 1, axis=1)
    weight = lax.dynamic_slice_in_dim(routes, me + experts, 1, axis=1)
    rows_x = jnp.where(on > 0.0, all_x.reshape(rows, width), jnp.bfloat16(0))
    rows_g = (weight * all_g.reshape(rows, width).astype(jnp.float32)).astype(jnp.bfloat16)
    gate_w = w_gate[0]
    up_w = w_up[0]
    down_w = w_down[0]
    pre_gate = jnp.dot(rows_x, gate_w, preferred_element_type=jnp.float32)
    pre_up = jnp.dot(rows_x, up_w, preferred_element_type=jnp.float32)
    act, slope = silu_parts(pre_gate)
    hidden = (act * pre_up).astype(jnp.bfloat16)
    d_hidden = jnp.dot(rows_g, down_w.T, preferred_element_type=jnp.float32)
    d_gate = (d_hidden * pre_up * slope).astype(jnp.bfloat16)
    d_up = (d_hidden * act).astype(jnp.bfloat16)
    part = jnp.dot(d_gate, gate_w.T, preferred_element_type=jnp.float32)
    part = part + jnp.dot(d_up, up_w.T, preferred_element_type=jnp.float32)
    part = lax.optimization_barrier(part.astype(jnp.bfloat16))
    summed = lax.psum_scatter(
        part.reshape(devices, tok_rows, width), BOTH, scatter_dimension=0, tiled=True
    )
    grad_down = jnp.dot(hidden.T, rows_g, preferred_element_type=jnp.float32).astype(jnp.bfloat16)
    grad_gate = jnp.dot(rows_x.T, d_gate, preferred_element_type=jnp.float32).astype(jnp.bfloat16)
    grad_up = jnp.dot(rows_x.T, d_up, preferred_element_type=jnp.float32).astype(jnp.bfloat16)
    return (summed[0].astype(jnp.float32), grad_gate[None], grad_up[None], grad_down[None])


def solution(mesh):
    tokens = P(BOTH, None)
    wide = P("local", None, "group")
    tall = P("local", "group", None)
    return jax.shard_map(
        body,
        mesh=mesh,
        in_specs=(tokens, tokens, tokens, tokens, wide, wide, tall),
        out_specs=(tokens, wide, wide, tall),
        check_vma=False,
    )
```

time: 242 us -> 309 us (1.28)
  waiting for transfers between devices: 83.8 us -> 181 us
  local copies, waits for them, and re-layouts: 36.2 us -> 23.4 us
  blocking collectives: 56.1 us -> 44 us
  other arithmetic: 0.46 us -> 11 us
  matrix products: 45.7 us -> 35.6 us
  starting transfers between devices: 4.73 us -> 0.11 us
    reduce_scatter x0 -> x1, waiting for transfers between devices: none -> 116 us  [body(): lax.psum_scatter(part.reshape(devices, tok_rows, width), BOTH, scatter_di...]
    all_to_all x2 -> x0, blocking collectives: 56.1 us -> none  [the longest x1 29.9 us: body(): lax.all_to_all(x_bins, 'local', split_axis=0, concat_axis=0, tiled=True)]
    all_gather x0 -> x1, blocking collectives: none -> 44 us  [body(): lax.all_gather(jnp.concatenate([on, weight], axis=1)[None], BOTH, axis=0,...]
    unnamed x4 -> x3, waiting for transfers between devices: 40.9 us -> 1.39 us
    all_gather x2, waiting for transfers between devices: 34.6 us -> 63.6 us  [the longest x1 44.8 us: body(): all_g = lax.all_gather(cotangent[None], BOTH, axis=0, tiled=True)]
    all_gather x2 -> x0, local copies, waits for them, and re-layouts: 10.3 us -> none  [the longest x1 5.15 us: body(): lax.all_gather(first[0][None], 'group', axis=0, tiled=True)]
    all_to_all x1 -> x0, waiting for transfers between devices: 8.38 us -> none  [body(): lax.all_to_all(summed_here[0].astype(jnp.bfloat16), 'local', split_axis=0...]
    reshape x5 -> x1, local copies, waits for them, and re-layouts: 9.77 us -> 2.75 us  [body(): part.reshape(devices, tok_rows, width)]
  transfers between devices with their start and end apart: 4 -> 3, of which waited for: 4 -> 3; matrix products, arithmetic and copies ran while one was open for 16% -> 14% of each run, Pallas kernels for 0% -> 0%
where the time goes in v1:
time: 309 us
  waiting for transfers between devices  181 us (59%)
  blocking collectives  44 us (14%)
  matrix products  35.6 us (12%)
  local copies, waits for them, and re-layouts  23.4 us (8%)
  between operations  14 us (5%)
  other arithmetic  11 us (4%)
    reduce_scatter x1, waiting for transfers between devices, body(): lax.psum_scatter(part.reshape(devices, tok_rows, width), BOTH, scatter_di...  116 us
    all_gather x1, waiting for transfers between devices, body(): all_g = lax.all_gather(cotangent[None], BOTH, axis=0, tiled=True)  44.8 us
    all_gather x1, blocking collectives, body(): lax.all_gather(jnp.concatenate([on, weight], axis=1)[None], BOTH, axis=0,...  44 us
    all_gather x1, waiting for transfers between devices, body(): all_x = lax.all_gather(features[None], BOTH, axis=0, tiled=True)  18.8 us
    dot_general x1, matrix products, body(): d_hidden = jnp.dot(rows_g, down_w.T, preferred_element_type=jnp.float32)  6.64 us
  transfers between devices with their start and end apart: 3, of which 3 were waited for; matrix products, arithmetic and copies ran while one was open for 14% of the time, Pallas kernels for 0%

profile of v1, /device:TPU:0, one launch (start us, length us, event | category | flops | bytes accessed | tf_op | source)
XLA Modules:
  0.0 309.0 jit_solution(17703085022566899046)
XLA Ops:
  7.2 0.0 all-gather.11.cloned.1.call-start
  7.2 0.7 all-gather.11.cloned.1.call-update
  7.9 0.0 all-gather.9.cloned.1.call-start
  7.9 0.7 all-gather.9.cloned.1.call-update
  8.6 0.0 reduce-scatter.2.cloned.1.call-start
  8.7 0.8 copy.17
  9.5 0.8 copy.18
  10.2 0.1 convert_reduce_fusion
  10.3 0.1 maximum_bitcast_fusion
  10.4 44.0 %all-gather.3 = f32[32,6,16]{2,1,0:T(8,128)S(1)} all-gather(f32[1,6,16]{2,1,0:T(8,128)S(1)} %maximum_bitcast_fusion), channel_id=2, replica_groups=mesh['group'=4,'local'=8] {'group','local'}, dimensions={0}, use_global_device_ids=true | all-gather | bytes 12672 | tf_op jit(solution)/shard_map/all_gather | solution.py:22
  54.5 0.2 fusion.15
  54.7 0.1 broadcast_in_dim.57
  54.8 0.4 copy-done.8
  55.2 0.2 dynamic-slice_reduce_fusion
  55.3 0.0 copy-start.6
  55.4 0.1 mul.38
  55.5 18.8 %all-gather.11.cloned.1.call-done = bf16[32,6,7168]{2,1,0:T(8,128)(2,1)} async-done(((bf16[1,6,7168]{2,1,0:T(8,128)(2,1)}), bf16[32,6,7168]{2,1,0:T(8,128)(2,1)}) %all-gather.11.cloned.1.call-update) | async-done | bytes 2752528 | tf_op jit(solution)/shard_map/all_gather | solution.py:23
  74.3 0.0 copy-done.6
  74.3 4.3 %broadcast_select_fusion = bf16[32,6,7168]{2,1,0:T(8,128)(2,1)} fusion(bf16[32,6,7168]{2,1,0:T(8,128)(2,1)} %all-gather.11.cloned.1.call-done, pred[32,6]{1,0:T(8,128)(4,1)S(1)} %broadcast_in_dim.57), kind=kLoop, calls=%fused_computation.19 | loop fusion | flops 1376256 | bytes 5505216 | tf_op jit(solution)/shard_map/jit(_where)/select_n | solution.py:29
  78.5 4.8 %select_n.24 = bf16[192,7168]{1,0:T(8,128)(2,1)} reshape(bf16[32,6,7168]{2,1,0:T(8,128)(2,1)} %broadcast_select_fusion) | data formatting | bytes 5505024 | tf_op jit(solution)/shard_map/jit(_where)/select_n | solution.py:29
  83.3 5.7 %fusion.6 = f32[192,512]{1,0:T(8,128)S(1)} fusion(bf16[192,7168]{1,0:T(8,128)(2,1)} %select_n.24, bf16[1,7168,512]{2,1,0:T(8,128)(2,1)} %param.11), kind=kOutput, calls=%fused_computation.10 | convolution fusion | flops 1409286144 | bytes 10485760 | tf_op jit(solution)/shard_map/dot_general | solution.py:34
  89.0 0.0 slice-done.4
  89.1 0.0 slice-done.5
  89.1 0.3 copy-done
  89.4 2.4 fusion.9
  91.8 44.8 %all-gather.9.cloned.1.call-done = bf16[32,6,7168]{2,1,0:T(8,128)(2,1)} async-done(((bf16[1,6,7168]{2,1,0:T(8,128)(2,1)}), bf16[32,6,7168]{2,1,0:T(8,128)(2,1)}) %all-gather.9.cloned.1.call-update) | async-done | bytes 2752528 | tf_op jit(solution)/shard_map/all_gather | solution.py:24
  136.6 4.8 %multiply_convert_fusion = bf16[32,6,7168]{2,1,0:T(8,128)(2,1)} fusion(f32[32,6]{1,0:T(8,128)S(1)} %mul.38, bf16[32,6,7168]{2,1,0:T(8,128)(2,1)} %all-gather.9.cloned.1.call-done), kind=kLoop, calls=%fused_computation.17 | loop fusion | flops 4128768 | bytes 5505792 | tf_op jit(solution)/shard_map/convert_element_type | solution.py:30
  141.3 4.8 %convert_element_type.50 = bf16[192,7168]{1,0:T(8,128)(2,1)} reshape(bf16[32,6,7168]{2,1,0:T(8,128)(2,1)} %multiply_convert_fusion) | data formatting | bytes 5505024 | tf_op jit(solution)/shard_map/convert_element_type | solution.py:30
  146.1 6.6 %multiply_convert_fusion.4 = (bf16[192,512]{1,0:T(8,128)(2,1)S(1)}, bf16[192,512]{1,0:T(8,128)(2,1)S(1)}) fusion(f32[192,512]{1,0:T(8,128)S(1)} %fusion.6, f32[192,512]{1,0:T(8,128)} %fusion.9, bf16[192,7168]{1,0:T(8,128)(2,1)} %convert_element_type.50, bf16[1,512,7168]{2,1,0:T(8,128)(2,1)} %param.13), kind=kOutput, calls=%fused_computation.23 | convolution fusion | flops 1410564096 | bytes 11272192 | tf_op jit(solution)/shard_map/dot_general | solution.py:38
  152.8 0.0 copy-start.4
  152.8 0.0 copy-start.2
  152.8 0.0 slice-start.7
  152.8 2.5 fusion.4
  155.4 0.0 copy-done.4
  155.4 2.5 fusion.3
  157.9 2.7 reshape.43
  160.7 0.0 reduce-scatter.2.cloned.1.call-update
  160.7 3.2 %reshape.62 = bf16[192,7168]{1,0:T(8,128)(2,1)S(1)} reshape(bf16[32,6,7168]{2,1,0:T(8,128)(2,1)} %all-gather.11.cloned.1.call-done) | data formatting | bytes 5505024
  163.9 0.0 copy-start.3
  164.0 0.0 copy-start.9
  164.0 5.2 %reshape.63 = f32[192,7168]{1,0:T(8,128)} reshape(bf16[32,6,7168]{2,1,0:T(8,128)(2,1)} %all-gather.9.cloned.1.call-done) | data formatting | bytes 8257536 | tf_op jit(solution)/shard_map/convert_element_type | solution.py:30
  169.2 0.0 slice-start
  169.2 5.3 %fusion.1 = bf16[1,7168,512]{2,1,0:T(8,128)(2,1)} fusion(bf16[192,512]{1,0:T(8,128)(2,1)S(1)} %copy-done.3, bf16[192,7168]{1,0:T(8,128)(2,1)S(1)} %reshape.62, pred[192]{0:T(512)(128)(4,1)S(1)} %copy-done.9), kind=kOutput, calls=%fused_computation.4 | convolution fusion | flops 1414332416 | bytes 10289344 | tf_op jit(solution)/shard_map/dot_general | solution.py:49
  174.5 5.3 %fusion = bf16[1,7168,512]{2,1,0:T(8,128)(2,1)} fusion(bf16[192,512]{1,0:T(8,128)(2,1)S(1)} %copy-done.5, bf16[192,7168]{1,0:T(8,128)(2,1)S(1)} %reshape.62, pred[192]{0:T(512)(128)(4,1)S(1)} %copy-done.9), kind=kOutput, calls=%fused_computation.3 | convolution fusion | flops 1414332416 | bytes 10289344 | tf_op jit(solution)/shard_map/dot_general | solution.py:48
  179.8 0.0 copy-done.7
  179.8 5.2 %fusion.2 = bf16[1,512,7168]{2,1,0:T(8,128)(2,1)} fusion(f32[192,7168]{1,0:T(8,128)S(1)} %bitcast.36, f32[192]{0:T(256)S(1)} %copy-done.7, f32[192,512]{1,0:T(8,128)S(1)} %copy-done.1, f32[192,512]{1,0:T(8,128)S(1)} %fusion.6), kind=kOutput, calls=%fused_computation.5 | convolution fusion | flops 1416298496 | bytes 13632256 | tf_op jit(solution)/shard_map/dot_general | solution.py:47
  185.1 115.8 %reduce-scatter.2.cloned.1.call-done = bf16[1,6,7168]{2,1,0:T(8,128)(2,1)} async-done(((bf16[32,6,7168]{2,1,0:T(8,128)(2,1)}), bf16[1,6,7168]{2,1,0:T(8,128)(2,1)}) %reduce-scatter.2.cloned.1.call-update) | async-done | bytes 86032 | tf_op jit(solution)/shard_map/reduce_scatter | solution.py:44
  300.8 1.6 bitcast_convert_fusion
  (27 shorter events, 0.1 us)
Async XLA Ops:
  7.2 67.1 %all-gather.11.cloned.1.call-start = ((), (), s32[]{:S(2)}) async-start(), calls=%async_computation.3 | async-start | bytes 3784704 | tf_op jit(solution)/shard_map/all_gather | solution.py:23
  7.9 128.7 %all-gather.9.cloned.1.call-start = ((), (), s32[]{:S(2)}) async-start(), calls=%async_computation.2 | async-start | bytes 3784704 | tf_op jit(solution)/shard_map/all_gather | solution.py:24
  8.6 292.2 %reduce-scatter.2.cloned.1.call-start = ((), (), s32[]{:S(2)}) async-start(), calls=%async_computation.1 | async-start | bytes 3784704 | tf_op jit(solution)/shard_map/reduce_scatter | solution.py:44
  54.6 0.5 copy-start.8
  55.3 18.9 %copy-start.6 = (f32[192]{0:T(256)}, f32[192]{0:T(256)S(1)}, u32[]{:S(2)}) copy-start(f32[192]{0:T(256)S(1)} %dynamic-slice_reduce_fusion) | copy-start | bytes 2308
  78.5 10.5 %slice-start.4 = ((s8[7340032]{0:T(1024)(128)(4,1)}), s8[3145728]{0:T(1024)(128)(4,1)S(1)}, s32[]{:S(2)}) async-start(s8[7340032]{0:T(1024)(128)(4,1)} %bitcast.39), calls=%async_computation.8 | async-start | bytes 6291456
  83.3 5.7 %slice-start.5 = ((s8[7340032]{0:T(1024)(128)(4,1)}), s8[4194304]{0:T(1024)(128)(4,1)S(1)}, s32[]{:S(2)}) async-start(s8[7340032]{0:T(1024)(128)(4,1)} %bitcast.39), calls=%async_computation.9 | async-start | bytes 8388608
  83.3 6.1 %copy-start = (bf16[192,7168]{1,0:T(8,128)(2,1)S(1)}, bf16[192,7168]{1,0:T(8,128)(2,1)}, u32[]{:S(2)}) copy-start(bf16[192,7168]{1,0:T(8,128)(2,1)} %select_n.24) | copy-start | bytes 8257540
  141.3 11.5 %slice-start.2 = ((s8[7340032]{0:T(1024)(128)(4,1)}), s8[3145728]{0:T(1024)(128)(4,1)S(1)}, s32[]{:S(2)}) async-start(s8[7340032]{0:T(1024)(128)(4,1)} %bitcast.37), calls=%async_computation.6 | async-start | bytes 6291456
  146.1 6.7 %slice-start.3 = ((s8[7340032]{0:T(1024)(128)(4,1)}), s8[4194304]{0:T(1024)(128)(4,1)S(1)}, s32[]{:S(2)}) async-start(s8[7340032]{0:T(1024)(128)(4,1)} %bitcast.37), calls=%async_computation.7 | async-start | bytes 8388608
  146.1 9.3 %slice-start.6 = ((s8[7340032]{0:T(1024)(128)(4,1)}), s8[4194304]{0:T(1024)(128)(4,1)S(1)}, s32[]{:S(2)}) async-start(s8[7340032]{0:T(1024)(128)(4,1)} %bitcast.41), calls=%async_computation.10 | async-start | bytes 8388608
  152.8 2.6 copy-start.4
  152.8 2.6 copy-start.2
  152.8 2.6 slice-start.7
  163.9 5.2 %copy-start.3 = (bf16[192,512]{1,0:T(8,128)(2,1)S(1)}, bf16[192,512]{1,0:T(8,128)(2,1)}, u32[]{:S(2)}) copy-start(bf16[192,512]{1,0:T(8,128)(2,1)} %copy-done.2) | copy-start | bytes 589828
  164.0 5.2 %copy-start.9 = (pred[192]{0:T(512)(128)(4,1)S(1)}, pred[192]{0:T(512)(128)(4,1)}, u32[]{:S(2)}) copy-start(pred[192]{0:T(512)(128)(4,1)} %copy-done.8) | copy-start | bytes 580
  169.2 5.3 %copy-start.5 = (bf16[192,512]{1,0:T(8,128)(2,1)S(1)}, bf16[192,512]{1,0:T(8,128)(2,1)}, u32[]{:S(2)}) copy-start(bf16[192,512]{1,0:T(8,128)(2,1)} %copy-done.4) | copy-start | bytes 589828
  169.2 10.6 %slice-start = ((s8[5505024]{0:T(1024)(128)(4,1)}), s8[4194304]{0:T(1024)(128)(4,1)S(1)}, s32[]{:S(2)}) async-start(s8[5505024]{0:T(1024)(128)(4,1)} %bitcast.35), calls=%async_computation.4 | async-start | bytes 8388608
  174.5 5.3 %slice-start.1 = ((s8[5505024]{0:T(1024)(128)(4,1)}), s8[1310720]{0:T(1024)(128)(4,1)S(1)}, s32[]{:S(2)}) async-start(s8[5505024]{0:T(1024)(128)(4,1)} %bitcast.35), calls=%async_computation.5 | async-start | bytes 2621440
  174.5 5.3 %copy-start.1 = (f32[192,512]{1,0:T(8,128)S(1)}, f32[192,512]{1,0:T(8,128)}, u32[]{:S(2)}) copy-start(f32[192,512]{1,0:T(8,128)} %fusion.9) | copy-start | bytes 1179652
  174.5 5.3 %copy-start.7 = (f32[192]{0:T(256)S(1)}, f32[192]{0:T(256)}, u32[]{:S(2)}) copy-start(f32[192]{0:T(256)} %copy-done.6) | copy-start | bytes 2308
Sparse Core Ops, SparseCore 0:
  10.8 63.3 all-gather.10
  77.1 59.4 all-gather.8
  160.8 139.9 reduce-scatter.1

commit v2 on v1

v2 whole, which is shorter than its diff:
```python
import functools

import jax
import jax.numpy as jnp
from jax import lax
from jax.experimental import pallas as pl
from jax.experimental.pallas import tpu as pltpu
from jax.sharding import PartitionSpec as P

BOTH = ("group", "local")
MESH = pl.DeviceIdType.MESH
ROWS = 8
EXTRA = 128


def place(groups, local):
    me_g, me_l = lax.axis_index("group"), lax.axis_index("local")
    z, core = me_l // 2, me_l % 2
    zs = local // 2
    g_at = lambda d: lax.rem(me_g + d, groups)
    z_at = lambda d: lax.rem(z + d, zs)
    sibling = (me_g, z * 2 + 1 - core)
    by_group = lambda d: (g_at(d), me_l)
    by_z = lambda d: (me_g, z_at(d) * 2 + core)
    return core, zs, g_at, z_at, sibling, by_group, by_z


def greet(groups, zs, sibling, by_group, by_z):
    peers = [sibling]
    peers += [by_group(d) for d in range(1, groups)]
    peers += [by_z(d) for d in range(1, zs)]
    barrier = pltpu.get_barrier_semaphore()
    for peer in peers:
        pl.semaphore_signal(barrier, inc=1, device_id=peer, device_id_type=MESH)
    pl.semaphore_wait(barrier, len(peers))


def gather_kernel(groups, local, x_in, g_in, x_out, g_out, own_sem, send_sem, recv_sem):
    core, zs, g_at, z_at, sibling, by_group, by_z = place(groups, local)
    pairs = ((x_in, x_out), (g_in, g_out))
    slot = lambda d, e, c: g_at(d) * local + z_at(e) * 2 + c
    greet(groups, zs, sibling, by_group, by_z)
    mine = slot(0, 0, core)
    sent = []

    def send(a, src, at, msg, peer):
        copy = pltpu.make_async_remote_copy(
            src_ref=src, dst_ref=pairs[a][1].at[at], send_sem=send_sem.at[a, msg],
            recv_sem=recv_sem.at[a, at], device_id=peer, device_id_type=MESH,
        )
        copy.start()
        sent.append(copy)

    def arrived(a, at):
        block = pairs[a][1].at[at]
        pltpu.make_async_remote_copy(
            src_ref=block, dst_ref=block, send_sem=send_sem.at[a, 0],
            recv_sem=recv_sem.at[a, at], device_id=sibling, device_id_type=MESH,
        ).wait_recv()

    first_group = zs - 1
    first_core = first_group + zs * (groups - 1)
    keeps = []
    for a in range(2):
        keep = pltpu.make_async_copy(pairs[a][0], pairs[a][1].at[mine], own_sem.at[a])
        keep.start()
        keeps.append(keep)
        for e in range(1, zs):
            send(a, pairs[a][0], mine, e - 1, by_z(e))
        for d in range(1, groups):
            send(a, pairs[a][0], mine, first_group + d - 1, by_group(d))
        send(a, pairs[a][0], mine, first_core, sibling)
    for a in range(2):
        for e in range(1, zs):
            at = slot(0, e, core)
            arrived(a, at)
            for d in range(1, groups):
                send(a, pairs[a][1].at[at], at, first_group + e * (groups - 1) + d - 1, by_group(d))
            send(a, pairs[a][1].at[at], at, first_core + e, sibling)
    for a in range(2):
        for e in range(zs):
            for d in range(1, groups):
                at = slot(d, e, core)
                arrived(a, at)
                send(a, pairs[a][1].at[at], at, first_core + d * zs + e, sibling)
    for a in range(2):
        for d in range(groups):
            for e in range(zs):
                arrived(a, slot(d, e, 1 - core))
    for copy in sent:
        copy.wait_send()
    for keep in keeps:
        keep.wait()


def reduce_kernel(
    groups, local, part, out, recv_core, sum_core, recv_group, sum_z, recv_z,
    send1, got1, send2, got2, send3, got3,
):
    core, zs, g_at, z_at, sibling, by_group, by_z = place(groups, local)
    slot = lambda d, e, c: g_at(d) * local + z_at(e) * 2 + c
    greet(groups, zs, sibling, by_group, by_z)
    f32 = jnp.float32
    order = [(d, e) for e in list(range(1, zs)) + [0] for d in list(range(1, groups)) + [0]]

    def send(src, dst, s_sem, r_sem, peer):
        copy = pltpu.make_async_remote_copy(
            src_ref=src, dst_ref=dst, send_sem=s_sem, recv_sem=r_sem,
            device_id=peer, device_id_type=MESH,
        )
        copy.start()
        return copy

    first = {}
    for d, e in order:
        k = d * zs + e
        first[k] = send(
            part.at[slot(d, e, 1 - core)], recv_core.at[k], send1.at[k], got1.at[k], sibling
        )
    second = {}
    for d, e in order:
        if d == 0:
            continue
        k = d * zs + e
        first[k].wait_recv()
        both = part[slot(d, e, core)].astype(f32) + recv_core[k].astype(f32)
        sum_core[k - zs] = both.astype(sum_core.dtype)
        second[k] = send(
            sum_core.at[k - zs], recv_group.at[k - zs], send2.at[k - zs], got2.at[k - zs], by_group(d)
        )
    third = []
    for e in list(range(1, zs)) + [0]:
        first[e].wait_recv()
        total = part[slot(0, e, core)].astype(f32) + recv_core[e].astype(f32)
        for d in range(1, groups):
            k = d * zs + e
            second[k].wait_recv()
            total = total + recv_group[k - zs].astype(f32)
        if e == 0:
            out[...] = total
        else:
            sum_z[e - 1] = total.astype(sum_z.dtype)
            third.append(
                send(sum_z.at[e - 1], recv_z.at[e - 1], send3.at[e - 1], got3.at[e - 1], by_z(e))
            )
    for e in range(1, zs):
        third[e - 1].wait_recv()
        out[...] += recv_z[e - 1].astype(f32)
    for copy in [*first.values(), *second.values(), *third]:
        copy.wait_send()


def gather(groups, local, x, g):
    n = groups * local
    zs = local // 2
    messages = zs - 1 + zs * (groups - 1) + zs * groups
    anywhere = pl.BlockSpec(memory_space=pl.ANY)
    return pl.pallas_call(
        functools.partial(gather_kernel, groups, local),
        out_shape=(
            jax.ShapeDtypeStruct((n,) + x.shape, x.dtype),
            jax.ShapeDtypeStruct((n,) + g.shape, g.dtype),
        ),
        in_specs=[anywhere] * 2,
        out_specs=(anywhere, anywhere),
        scratch_shapes=[
            pltpu.SemaphoreType.DMA((2,)),
            pltpu.SemaphoreType.DMA((2, messages)),
            pltpu.SemaphoreType.DMA((2, n)),
        ],
        compiler_params=pltpu.CompilerParams(collective_id=0, has_side_effects=True),
        name="gather",
    )(x, g)


def reduce(groups, local, part):
    zs = local // 2
    block = part.shape[1:]
    slots = lambda k: pltpu.VMEM((k,) + block, part.dtype)
    near, far = zs * groups, zs * (groups - 1)
    dma = pltpu.SemaphoreType.DMA
    return pl.pallas_call(
        functools.partial(reduce_kernel, groups, local),
        out_shape=jax.ShapeDtypeStruct(block, jnp.float32),
        in_specs=[pl.BlockSpec(memory_space=pltpu.VMEM)],
        out_specs=pl.BlockSpec(memory_space=pltpu.VMEM),
        scratch_shapes=[
            slots(near), slots(far), slots(far), slots(zs - 1), slots(zs - 1),
            dma((near,)), dma((near,)), dma((far,)), dma((far,)), dma((zs - 1,)), dma((zs - 1,)),
        ],
        compiler_params=pltpu.CompilerParams(
            collective_id=1, has_side_effects=True, vmem_limit_bytes=50 * 2**20
        ),
        name="reduce",
    )(part)


def silu_parts(pre):
    sig = jax.nn.sigmoid(pre)
    return (pre * sig, sig * (1.0 + pre * (1.0 - sig)))


def body(features, cotangent, expert_ids, gates, w_gate, w_up, w_down):
    local = lax.axis_size("local")
    groups = lax.axis_size("group")
    tok_rows, width = features.shape
    rows = groups * local * ROWS
    pad = ROWS - tok_rows
    hits = expert_ids[..., None] == jnp.arange(local, dtype=jnp.int32)
    weight = jnp.sum(jnp.where(hits, gates[..., None], 0.0), axis=1)
    high = lax.reduce_precision(weight, 8, 7)
    middle = lax.reduce_precision(weight - high, 8, 7)
    low = weight - high - middle
    terms = jnp.concatenate([high, middle, low], axis=1).astype(jnp.bfloat16)
    terms = jnp.pad(terms, ((0, 0), (0, EXTRA - 3 * local)))
    x = jnp.pad(features, ((0, pad), (0, 0)))
    g = jnp.pad(jnp.concatenate([cotangent, terms], axis=1), ((0, pad), (0, 0)))
    all_x, all_g = gather(groups, local, x, g)
    rows_x = all_x.reshape(rows, width)
    all_g = all_g.reshape(rows, width + EXTRA)
    terms = all_g[:, width : width + 3 * local].astype(jnp.float32).reshape(rows, 3, local)
    mine = jnp.arange(local) == lax.axis_index("local")
    terms = jnp.sum(jnp.where(mine, terms, 0.0), axis=2)
    weight = (terms[:, 0] + terms[:, 1] + terms[:, 2])[:, None]
    rows_g = (weight * all_g[:, :width].astype(jnp.float32)).astype(jnp.bfloat16)
    gate_w = w_gate[0]
    up_w = w_up[0]
    down_w = w_down[0]
    pre_gate = jnp.dot(rows_x, gate_w, preferred_element_type=jnp.float32)
    pre_up = jnp.dot(rows_x, up_w, preferred_element_type=jnp.float32)
    act, slope = silu_parts(pre_gate)
    hidden = (act * pre_up).astype(jnp.bfloat16)
    d_hidden = jnp.dot(rows_g, down_w.T, preferred_element_type=jnp.float32)
    d_gate = (d_hidden * pre_up * slope).astype(jnp.bfloat16)
    d_up = (d_hidden * act).astype(jnp.bfloat16)
    part = jnp.dot(d_gate, gate_w.T, preferred_element_type=jnp.float32)
    part = part + jnp.dot(d_up, up_w.T, preferred_element_type=jnp.float32)
    part = part.astype(jnp.bfloat16).reshape(groups * local, ROWS, width)
    summed = reduce(groups, local, part)
    grad_down = jnp.dot(hidden.T, rows_g, preferred_element_type=jnp.float32).astype(jnp.bfloat16)
    grad_gate = jnp.dot(rows_x.T, d_gate, preferred_element_type=jnp.float32).astype(jnp.bfloat16)
    grad_up = jnp.dot(rows_x.T, d_up, preferred_element_type=jnp.float32).astype(jnp.bfloat16)
    return (summed[:tok_rows], grad_gate[None], grad_up[None], grad_down[None])


def solution(mesh):
    tokens = P(BOTH, None)
    wide = P("local", None, "group")
    tall = P("local", "group", None)
    return jax.shard_map(
        body,
        mesh=mesh,
        in_specs=(tokens, tokens, tokens, tokens, wide, wide, tall),
        out_specs=(tokens, wide, wide, tall),
        check_vma=False,
    )
```

time: 309 us -> 132 us (0.43)
  waiting for transfers between devices: 181 us -> 0 us
  Pallas kernels: 0 us -> 80.8 us
  blocking collectives: 44 us -> 0 us
  local copies, waits for them, and re-layouts: 23.4 us -> 4.73 us
  between operations: 14 us -> 0.75 us
  other arithmetic: 11 us -> 2.02 us
  matrix products: 35.6 us -> 43.5 us
    reduce_scatter x1 -> x0, waiting for transfers between devices: 116 us -> none  [body(): lax.psum_scatter(part.reshape(devices, tok_rows, width), BOTH, scatter_di...]
    pallas_call x0 -> x2, Pallas kernels: none -> 80.8 us  [the longest x1 49.9 us: gather(): pl.pallas_call(functools.partial(gather_kernel, groups, local), out_shape...]
    all_gather x2 -> x0, waiting for transfers between devices: 63.6 us -> none  [the longest x1 44.8 us: body(): all_g = lax.all_gather(cotangent[None], BOTH, axis=0, tiled=True)]
    all_gather x1 -> x0, blocking collectives: 44 us -> none  [body(): lax.all_gather(jnp.concatenate([on, weight], axis=1)[None], BOTH, axis=0,...]
    convert_element_type x2 -> x0, local copies, waits for them, and re-layouts: 9.98 us -> none  [the longest x1 5.21 us: body(): all_g.reshape(rows, width).astype(jnp.float32)]
    convert_element_type x2 -> x0, other arithmetic: 6.39 us -> none  [the longest x1 4.79 us: body(): (weight * all_g.reshape(rows, width).astype(jnp.float32)).astype(jnp.bflo...]
    select_n x1 -> x0, local copies, waits for them, and re-layouts: 4.77 us -> none  [body(): rows_x = jnp.where(on > 0.0, all_x.reshape(rows, width), jnp.bfloat16(0))]
    select_n x1 -> x0, other arithmetic: 4.29 us -> none  [body(): rows_x = jnp.where(on > 0.0, all_x.reshape(rows, width), jnp.bfloat16(0))]
  transfers between devices with their start and end apart: 3 -> 0, of which waited for: 3 -> 0; matrix products, arithmetic and copies ran while one was open for 14% -> 0% of each run, Pallas kernels for 0% -> 0%
where the time goes in v2:
time: 132 us
  Pallas kernels  80.8 us (61%)
  matrix products  43.5 us (33%)
  local copies, waits for them, and re-layouts  4.73 us (4%)
  other arithmetic  2.02 us (2%)
    pallas_call x1, Pallas kernels, gather(): pl.pallas_call(functools.partial(gather_kernel, groups, local), out_shape...  49.9 us
    pallas_call x1, Pallas kernels, reduce(): pl.pallas_call(functools.partial(reduce_kernel, groups, local), out_shape...  31 us
    dot_general x1, matrix products, body(): pre_gate = jnp.dot(rows_x, gate_w, preferred_element_type=jnp.float32)  7.19 us
    dot_general x1, matrix products, body(): d_hidden = jnp.dot(rows_g, down_w.T, preferred_element_type=jnp.float32)  6.56 us
    dot_general x1, matrix products, body(): part = part + jnp.dot(d_up, up_w.T, preferred_element_type=jnp.float32)  5.62 us
    dot_general x1, matrix products, body(): jnp.dot(rows_x.T, d_gate, preferred_element_type=jnp.float32)  5.37 us
    dot_general x1, matrix products, body(): jnp.dot(hidden.T, rows_g, preferred_element_type=jnp.float32)  5.34 us
    dot_general x1, matrix products, body(): part = jnp.dot(d_gate, gate_w.T, preferred_element_type=jnp.float32)  5.29 us

profile of v2, /device:TPU:0, one launch (start us, length us, event | category | flops | bytes accessed | tf_op | source)
XLA Modules:
  0.0 131.8 jit_solution(5005189649170744704)
XLA Ops:
  0.6 1.6 %pad.12.x_in = bf16[8,7168]{1,0:T(8,128)(2,1)} pad(bf16[6,7168]{1,0:T(8,128)(2,1)} %param.7, bf16[]{:T(256)} %constant.2.clone.1), padding=0_2x0_0 | pad | bytes 200706 | tf_op jit(solution)/shard_map/jit(_pad)/pad | solution.py:216
  2.2 0.8 copy.17
  3.0 0.8 copy.16
  3.7 0.1 select_reduce_fusion
  3.8 0.1 fusion.29
  3.9 0.0 slice-start
  3.9 1.7 %fusion.21.g_in = bf16[8,7296]{1,0:T(8,128)(2,1)} fusion(bf16[6,128]{1,0:T(8,128)(2,1)S(1)} %fusion.29, bf16[6,7168]{1,0:T(8,128)(2,1)} %param.8), kind=kLoop, calls=%fused_computation.31 | loop fusion | flops 408576 | bytes 204288 | tf_op jit(solution)/shard_map/concatenate | solution.py:217
  5.7 49.9 %gather.1 = (bf16[32,8,7168]{2,1,0:T(8,128)(2,1)}, bf16[32,8,7296]{2,1,0:T(8,128)(2,1)}) custom-call(bf16[8,7168]{1,0:T(8,128)(2,1)} %pad.12.x_in, bf16[8,7296]{1,0:T(8,128)(2,1)} %fusion.21.g_in), custom_call_target="tpu_custom_call" | custom-call | tf_op jit(solution)/shard_map/gather/pallas_call | solution.py:158
  55.5 0.0 copy-start
  55.5 0.0 slice-start.1
  55.6 7.2 %fusion.7 = f32[256,512]{1,0:T(8,128)} fusion(bf16[1,7168,512]{2,1,0:T(8,128)(2,1)} %param.11, bf16[32,8,7168]{2,1,0:T(8,128)(2,1)} %get-tuple-element.7), kind=kOutput, calls=%fused_computation.11 | convolution fusion | flops 1879048192 | bytes 11534336 | tf_op jit(solution)/shard_map/dot_general | solution.py:229
  62.7 0.0 slice-done
  62.7 0.0 copy-done
  62.7 0.0 slice-done.1
  62.8 3.0 %fusion.10 = f32[256,512]{1,0:T(8,128)} fusion(bf16[1,7168,512]{2,1,0:T(8,128)(2,1)S(1)} %bitcast.44, bf16[32,8,7168]{2,1,0:T(8,128)(2,1)S(1)} %copy-done), kind=kOutput, calls=%fused_computation.14 | convolution fusion | flops 1879048192 | bytes 11534336 | tf_op jit(solution)/shard_map/dot_general | solution.py:230
  65.7 0.8 slice.24
  66.6 0.1 copy.19
  66.7 0.1 fusion.23
  66.8 6.6 %multiply_convert_fusion.4 = (bf16[256,512]{1,0:T(8,128)(2,1)S(1)}, bf16[256,512]{1,0:T(8,128)(2,1)S(1)}) fusion(f32[256,512]{1,0:T(8,128)} %fusion.7, f32[256,512]{1,0:T(8,128)} %fusion.10, bf16[1,512,7168]{2,1,0:T(8,128)(2,1)} %param.13, bf16[256,7296]{1,0:T(8,128)(2,1)} %bitcast.46, f32[256]{0:T(256)S(1)} %bitcast.48), kind=kOutput, calls=%fused_computation.24 | convolution fusion | flops 1886257152 | bytes 12583936 | tf_op jit(solution)/shard_map/dot_general | solution.py:233
  73.3 5.3 %fusion.5 = f32[256,7168]{1,0:T(8,128)S(1)} fusion(bf16[256,512]{1,0:T(8,128)(2,1)S(1)} %get-tuple-element.9, bf16[1,7168,512]{2,1,0:T(8,128)(2,1)} %param.11), kind=kOutput, calls=%fused_computation.9 | convolution fusion | flops 1879048192 | bytes 14942208 | tf_op jit(solution)/shard_map/dot_general | solution.py:236
  78.6 0.0 copy-start.1
  78.6 5.6 %fusion.4.part = bf16[32,8,7168]{2,1,0:T(8,128)(2,1)S(1)} fusion(f32[256,7168]{1,0:T(8,128)S(1)} %fusion.5, bf16[256,512]{1,0:T(8,128)(2,1)S(1)} %get-tuple-element.8, bf16[1,7168,512]{2,1,0:T(8,128)(2,1)} %param.12), kind=kOutput, calls=%fused_computation.8 | convolution fusion | flops 1882718208 | bytes 18612224 | tf_op jit(solution)/shard_map/dot_general | solution.py:237
  84.3 31.0 %reduce.1 = f32[8,7168]{1,0:T(8,128)S(1)} custom-call(bf16[32,8,7168]{2,1,0:T(8,128)(2,1)S(1)} %fusion.4.part), custom_call_target="tpu_custom_call" | custom-call | tf_op jit(solution)/shard_map/reduce/pallas_call | solution.py:182
  115.2 0.0 copy-done.1
  115.3 5.4 %fusion = bf16[1,7168,512]{2,1,0:T(8,128)(2,1)} fusion(bf16[256,512]{1,0:T(8,128)(2,1)S(1)} %get-tuple-element.9, bf16[32,8,7168]{2,1,0:T(8,128)(2,1)S(1)} %copy-done.1), kind=kOutput, calls=%fused_computation.3 | convolution fusion | flops 1882718208 | bytes 11272192 | tf_op jit(solution)/shard_map/dot_general | solution.py:241
  120.6 0.0 copy-start.2
  120.6 0.0 copy-start.3
  120.6 0.0 copy-start.4
  120.6 5.2 %fusion.1 = bf16[1,7168,512]{2,1,0:T(8,128)(2,1)} fusion(bf16[256,512]{1,0:T(8,128)(2,1)S(1)} %get-tuple-element.8, bf16[32,8,7168]{2,1,0:T(8,128)(2,1)S(1)} %copy-done.1), kind=kOutput, calls=%fused_computation.4 | convolution fusion | flops 1882718208 | bytes 11272192 | tf_op jit(solution)/shard_map/dot_general | solution.py:242
  125.8 0.0 copy-done.2
  125.8 0.0 copy-done.3
  125.8 0.0 copy-done.4
  125.8 5.3 %fusion.2 = bf16[1,512,7168]{2,1,0:T(8,128)(2,1)} fusion(bf16[256,7296]{1,0:T(8,128)(2,1)S(1)} %bitcast.47, f32[256]{0:T(256)S(1)} %bitcast.49, f32[256,512]{1,0:T(8,128)S(1)} %copy-done.4, f32[256,512]{1,0:T(8,128)S(1)} %copy-done.3), kind=kOutput, calls=%fused_computation.5 | convolution fusion | flops 1889009664 | bytes 12059648 | tf_op jit(solution)/shard_map/dot_general | solution.py:240
  131.1 0.7 copy.21
  (4 shorter events, 0.0 us)
Async XLA Ops:
  3.9 58.8 %slice-start = ((s8[7340032]{0:T(1024)(128)(4,1)}), s8[3145728]{0:T(1024)(128)(4,1)S(1)}, s32[]{:S(2)}) async-start(s8[7340032]{0:T(1024)(128)(4,1)} %bitcast.43), calls=%async_computation | async-start | bytes 6291456
  55.5 7.2 %copy-start = (bf16[32,8,7168]{2,1,0:T(8,128)(2,1)S(1)}, bf16[32,8,7168]{2,1,0:T(8,128)(2,1)}, u32[]{:S(2)}) copy-start(bf16[32,8,7168]{2,1,0:T(8,128)(2,1)} %get-tuple-element.7) | copy-start | bytes 11010052
  55.5 7.2 %slice-start.1 = ((s8[7340032]{0:T(1024)(128)(4,1)}), s8[4194304]{0:T(1024)(128)(4,1)S(1)}, s32[]{:S(2)}) async-start(s8[7340032]{0:T(1024)(128)(4,1)} %bitcast.43), calls=%async_computation.1 | async-start | bytes 8388608
  78.6 36.6 %copy-start.1 = (bf16[32,8,7168]{2,1,0:T(8,128)(2,1)S(1)}, bf16[32,8,7168]{2,1,0:T(8,128)(2,1)}, u32[]{:S(2)}) copy-start(bf16[32,8,7168]{2,1,0:T(8,128)(2,1)} %get-tuple-element.7) | copy-start | bytes 11010052
  120.6 5.2 %copy-start.2 = (bf16[32,8,7296]{2,1,0:T(8,128)(2,1)S(1)}, bf16[32,8,7296]{2,1,0:T(8,128)(2,1)}, u32[]{:S(2)}) copy-start(bf16[32,8,7296]{2,1,0:T(8,128)(2,1)} %get-tuple-element.6) | copy-start | bytes 11206660
  120.6 5.2 %copy-start.3 = (f32[256,512]{1,0:T(8,128)S(1)}, f32[256,512]{1,0:T(8,128)}, u32[]{:S(2)}) copy-start(f32[256,512]{1,0:T(8,128)} %fusion.7) | copy-start | bytes 1572868
  120.6 5.2 %copy-start.4 = (f32[256,512]{1,0:T(8,128)S(1)}, f32[256,512]{1,0:T(8,128)}, u32[]{:S(2)}) copy-start(f32[256,512]{1,0:T(8,128)} %fusion.10) | copy-start | bytes 1572868

commit v3 on v2

--- a/solution.py
+++ b/solution.py
@@ -18,6 +18,11 @@
     z, core = me_l // 2, me_l % 2
     zs = local // 2
     g_at = lambda d: lax.rem(me_g + d, groups)
+    if groups == 4:
+        across, along = me_g // 2, me_g % 2
+        g_at = lambda d: (
+            me_g, across * 2 + 1 - along, (1 - across) * 2 + along, (1 - across) * 2 + 1 - along
+        )[d]
     z_at = lambda d: lax.rem(z + d, zs)
     sibling = (me_g, z * 2 + 1 - core)
     by_group = lambda d: (g_at(d), me_l)
@@ -61,28 +66,45 @@
     first_group = zs - 1
     first_core = first_group + zs * (groups - 1)
     keeps = []
+    relayed = groups == 4
+    direct = range(1, 3 if relayed else groups)
+
+    def relay(a, at, d, e):
+        if relayed and d == 1 + e % 2:
+            send(a, pairs[a][1].at[at], at, first_group + e * (groups - 1) + 2, by_group(3 - d))
+
+    def pass_on(a, d, e):
+        at = slot(d, e, core)
+        arrived(a, at)
+        relay(a, at, d, e)
+        send(a, pairs[a][1].at[at], at, first_core + d * zs + e, sibling)
+
     for a in range(2):
         keep = pltpu.make_async_copy(pairs[a][0], pairs[a][1].at[mine], own_sem.at[a])
         keep.start()
         keeps.append(keep)
         for e in range(1, zs):
             send(a, pairs[a][0], mine, e - 1, by_z(e))
-        for d in range(1, groups):
+        for d in direct:
             send(a, pairs[a][0], mine, first_group + d - 1, by_group(d))
         send(a, pairs[a][0], mine, first_core, sibling)
     for a in range(2):
         for e in range(1, zs):
             at = slot(0, e, core)
             arrived(a, at)
-            for d in range(1, groups):
+            for d in direct:
                 send(a, pairs[a][1].at[at], at, first_group + e * (groups - 1) + d - 1, by_group(d))
             send(a, pairs[a][1].at[at], at, first_core + e, sibling)
+        for d in direct:
+            pass_on(a, d, 0)
+    for a in range(2):
+        for e in range(1, zs):
+            for d in direct:
+                pass_on(a, d, e)
     for a in range(2):
         for e in range(zs):
-            for d in range(1, groups):
-                at = slot(d, e, core)
-                arrived(a, at)
-                send(a, pairs[a][1].at[at], at, first_core + d * zs + e, sibling)
+            for d in range(3 if relayed else groups, groups):
+                pass_on(a, d, e)
     for a in range(2):
         for d in range(groups):
             for e in range(zs):
@@ -101,7 +123,7 @@
     slot = lambda d, e, c: g_at(d) * local + z_at(e) * 2 + c
     greet(groups, zs, sibling, by_group, by_z)
     f32 = jnp.float32
-    order = [(d, e) for e in list(range(1, zs)) + [0] for d in list(range(1, groups)) + [0]]
+    order = [(d, e) for e in list(range(1, zs)) + [0] for d in list(range(groups - 1, 0, -1)) + [0]]
 
     def send(src, dst, s_sem, r_sem, peer):
         copy = pltpu.make_async_remote_copy(
@@ -118,21 +140,36 @@
             part.at[slot(d, e, 1 - core)], recv_core.at[k], send1.at[k], got1.at[k], sibling
         )
     second = {}
-    for d, e in order:
-        if d == 0:
-            continue
+    relayed = groups == 4
+
+    def add_and_send(d, e, extra, peer):
         k = d * zs + e
         first[k].wait_recv()
         both = part[slot(d, e, core)].astype(f32) + recv_core[k].astype(f32)
+        if extra:
+            second[3 * zs + e].wait_recv()
+            both = both + recv_group[2 * zs + e].astype(f32)
         sum_core[k - zs] = both.astype(sum_core.dtype)
         second[k] = send(
-            sum_core.at[k - zs], recv_group.at[k - zs], send2.at[k - zs], got2.at[k - zs], by_group(d)
-        )
+            sum_core.at[k - zs], recv_group.at[k - zs], send2.at[k - zs], got2.at[k - zs], by_group(peer)
+        )
+
+    late = list(range(1, zs)) + [0]
+    if relayed:
+        for e in late:
+            add_and_send(3, e, False, 1 + e % 2)
+            add_and_send(1 + e % 2, e, False, 1 + e % 2)
+        for e in late:
+            add_and_send(2 - e % 2, e, True, 2 - e % 2)
+    else:
+        for d, e in order:
+            if d:
+                add_and_send(d, e, False, d)
     third = []
     for e in list(range(1, zs)) + [0]:
         first[e].wait_recv()
         total = part[slot(0, e, core)].astype(f32) + recv_core[e].astype(f32)
-        for d in range(1, groups):
+        for d in range(1, 3 if relayed else groups):
             k = d * zs + e
             second[k].wait_recv()
             total = total + recv_group[k - zs].astype(f32)

time: 132 us -> 131 us (level)
    pallas_call x1, Pallas kernels: 49.9 us -> 43.7 us  [gather(): pl.pallas_call(functools.partial(gather_kernel, groups, local), out_shape...]
    pallas_call x1, Pallas kernels: 31 us -> 35.8 us  [reduce(): pl.pallas_call(functools.partial(reduce_kernel, groups, local), out_shape...]
where the time goes in v3:
time: 131 us
  Pallas kernels  79.5 us (61%)
  matrix products  43.5 us (33%)
  local copies, waits for them, and re-layouts  4.73 us (4%)
  other arithmetic  2.02 us (2%)
    pallas_call x1, Pallas kernels, gather(): pl.pallas_call(functools.partial(gather_kernel, groups, local), out_shape...  43.7 us
    pallas_call x1, Pallas kernels, reduce(): pl.pallas_call(functools.partial(reduce_kernel, groups, local), out_shape...  35.8 us
    dot_general x1, matrix products, body(): pre_gate = jnp.dot(rows_x, gate_w, preferred_element_type=jnp.float32)  7.19 us
    dot_general x1, matrix products, body(): d_hidden = jnp.dot(rows_g, down_w.T, preferred_element_type=jnp.float32)  6.56 us
    dot_general x1, matrix products, body(): part = part + jnp.dot(d_up, up_w.T, preferred_element_type=jnp.float32)  5.62 us
    dot_general x1, matrix products, body(): jnp.dot(rows_x.T, d_gate, preferred_element_type=jnp.float32)  5.37 us
    dot_general x1, matrix products, body(): jnp.dot(hidden.T, rows_g, preferred_element_type=jnp.float32)  5.34 us
    dot_general x1, matrix products, body(): part = jnp.dot(d_gate, gate_w.T, preferred_element_type=jnp.float32)  5.28 us

profile of v3, /device:TPU:0, one launch (start us, length us, event | category | flops | bytes accessed | tf_op | source)
XLA Modules:
  0.0 130.5 jit_solution(12093265100843701899)
XLA Ops:
  0.6 1.6 %pad.12.x_in = bf16[8,7168]{1,0:T(8,128)(2,1)} pad(bf16[6,7168]{1,0:T(8,128)(2,1)} %param.7, bf16[]{:T(256)} %constant.2.clone.1), padding=0_2x0_0 | pad | bytes 200706 | tf_op jit(solution)/shard_map/jit(_pad)/pad | solution.py:253
  2.2 0.8 copy.17
  3.0 0.8 copy.16
  3.7 0.1 select_reduce_fusion
  3.8 0.1 fusion.29
  3.9 0.0 slice-start
  3.9 1.7 %fusion.21.g_in = bf16[8,7296]{1,0:T(8,128)(2,1)} fusion(bf16[6,128]{1,0:T(8,128)(2,1)S(1)} %fusion.29, bf16[6,7168]{1,0:T(8,128)(2,1)} %param.8), kind=kLoop, calls=%fused_computation.31 | loop fusion | flops 408576 | bytes 204288 | tf_op jit(solution)/shard_map/concatenate | solution.py:254
  5.7 43.7 %gather.1 = (bf16[32,8,7168]{2,1,0:T(8,128)(2,1)}, bf16[32,8,7296]{2,1,0:T(8,128)(2,1)}) custom-call(bf16[8,7168]{1,0:T(8,128)(2,1)} %pad.12.x_in, bf16[8,7296]{1,0:T(8,128)(2,1)} %fusion.21.g_in), custom_call_target="tpu_custom_call" | custom-call | tf_op jit(solution)/shard_map/gather/pallas_call | solution.py:195
  49.4 0.0 copy-start
  49.4 0.0 slice-start.1
  49.4 7.2 %fusion.7 = f32[256,512]{1,0:T(8,128)} fusion(bf16[1,7168,512]{2,1,0:T(8,128)(2,1)} %param.11, bf16[32,8,7168]{2,1,0:T(8,128)(2,1)} %get-tuple-element.7), kind=kOutput, calls=%fused_computation.11 | convolution fusion | flops 1879048192 | bytes 11534336 | tf_op jit(solution)/shard_map/dot_general | solution.py:266
  56.6 0.0 slice-done
  56.6 0.0 copy-done
  56.6 0.0 slice-done.1
  56.6 3.0 %fusion.10 = f32[256,512]{1,0:T(8,128)} fusion(bf16[1,7168,512]{2,1,0:T(8,128)(2,1)S(1)} %bitcast.44, bf16[32,8,7168]{2,1,0:T(8,128)(2,1)S(1)} %copy-done), kind=kOutput, calls=%fused_computation.14 | convolution fusion | flops 1879048192 | bytes 11534336 | tf_op jit(solution)/shard_map/dot_general | solution.py:267
  59.6 0.8 slice.24
  60.4 0.1 copy.19
  60.5 0.1 fusion.23
  60.6 6.6 %multiply_convert_fusion.4 = (bf16[256,512]{1,0:T(8,128)(2,1)S(1)}, bf16[256,512]{1,0:T(8,128)(2,1)S(1)}) fusion(f32[256,512]{1,0:T(8,128)} %fusion.7, f32[256,512]{1,0:T(8,128)} %fusion.10, bf16[1,512,7168]{2,1,0:T(8,128)(2,1)} %param.13, bf16[256,7296]{1,0:T(8,128)(2,1)} %bitcast.46, f32[256]{0:T(256)S(1)} %bitcast.48), kind=kOutput, calls=%fused_computation.24 | convolution fusion | flops 1886257152 | bytes 12583936 | tf_op jit(solution)/shard_map/dot_general | solution.py:270
  67.2 5.3 %fusion.5 = f32[256,7168]{1,0:T(8,128)S(1)} fusion(bf16[256,512]{1,0:T(8,128)(2,1)S(1)} %get-tuple-element.9, bf16[1,7168,512]{2,1,0:T(8,128)(2,1)} %param.11), kind=kOutput, calls=%fused_computation.9 | convolution fusion | flops 1879048192 | bytes 14942208 | tf_op jit(solution)/shard_map/dot_general | solution.py:273
  72.5 0.0 copy-start.1
  72.5 5.6 %fusion.4.part = bf16[32,8,7168]{2,1,0:T(8,128)(2,1)S(1)} fusion(f32[256,7168]{1,0:T(8,128)S(1)} %fusion.5, bf16[256,512]{1,0:T(8,128)(2,1)S(1)} %get-tuple-element.8, bf16[1,7168,512]{2,1,0:T(8,128)(2,1)} %param.12), kind=kOutput, calls=%fused_computation.8 | convolution fusion | flops 1882718208 | bytes 18612224 | tf_op jit(solution)/shard_map/dot_general | solution.py:274
  78.1 35.8 %reduce.1 = f32[8,7168]{1,0:T(8,128)S(1)} custom-call(bf16[32,8,7168]{2,1,0:T(8,128)(2,1)S(1)} %fusion.4.part), custom_call_target="tpu_custom_call" | custom-call | tf_op jit(solution)/shard_map/reduce/pallas_call | solution.py:219
  113.9 0.0 copy-done.1
  113.9 5.4 %fusion = bf16[1,7168,512]{2,1,0:T(8,128)(2,1)} fusion(bf16[256,512]{1,0:T(8,128)(2,1)S(1)} %get-tuple-element.9, bf16[32,8,7168]{2,1,0:T(8,128)(2,1)S(1)} %copy-done.1), kind=kOutput, calls=%fused_computation.3 | convolution fusion | flops 1882718208 | bytes 11272192 | tf_op jit(solution)/shard_map/dot_general | solution.py:278
  119.3 0.0 copy-start.2
  119.3 0.0 copy-start.3
  119.3 0.0 copy-start.4
  119.3 5.2 %fusion.1 = bf16[1,7168,512]{2,1,0:T(8,128)(2,1)} fusion(bf16[256,512]{1,0:T(8,128)(2,1)S(1)} %get-tuple-element.8, bf16[32,8,7168]{2,1,0:T(8,128)(2,1)S(1)} %copy-done.1), kind=kOutput, calls=%fused_computation.4 | convolution fusion | flops 1882718208 | bytes 11272192 | tf_op jit(solution)/shard_map/dot_general | solution.py:279
  124.5 0.0 copy-done.2
  124.5 0.0 copy-done.3
  124.5 0.0 copy-done.4
  124.5 5.3 %fusion.2 = bf16[1,512,7168]{2,1,0:T(8,128)(2,1)} fusion(bf16[256,7296]{1,0:T(8,128)(2,1)S(1)} %bitcast.47, f32[256]{0:T(256)S(1)} %bitcast.49, f32[256,512]{1,0:T(8,128)S(1)} %copy-done.4, f32[256,512]{1,0:T(8,128)S(1)} %copy-done.3), kind=kOutput, calls=%fused_computation.5 | convolution fusion | flops 1889009664 | bytes 12059648 | tf_op jit(solution)/shard_map/dot_general | solution.py:277
  129.8 0.7 copy.21
  (4 shorter events, 0.0 us)
Async XLA Ops:
  3.9 52.7 %slice-start = ((s8[7340032]{0:T(1024)(128)(4,1)}), s8[3145728]{0:T(1024)(128)(4,1)S(1)}, s32[]{:S(2)}) async-start(s8[7340032]{0:T(1024)(128)(4,1)} %bitcast.43), calls=%async_computation | async-start | bytes 6291456
  49.4 7.2 %copy-start = (bf16[32,8,7168]{2,1,0:T(8,128)(2,1)S(1)}, bf16[32,8,7168]{2,1,0:T(8,128)(2,1)}, u32[]{:S(2)}) copy-start(bf16[32,8,7168]{2,1,0:T(8,128)(2,1)} %get-tuple-element.7) | copy-start | bytes 11010052
  49.4 7.2 %slice-start.1 = ((s8[7340032]{0:T(1024)(128)(4,1)}), s8[4194304]{0:T(1024)(128)(4,1)S(1)}, s32[]{:S(2)}) async-start(s8[7340032]{0:T(1024)(128)(4,1)} %bitcast.43), calls=%async_computation.1 | async-start | bytes 8388608
  72.5 41.4 %copy-start.1 = (bf16[32,8,7168]{2,1,0:T(8,128)(2,1)S(1)}, bf16[32,8,7168]{2,1,0:T(8,128)(2,1)}, u32[]{:S(2)}) copy-start(bf16[32,8,7168]{2,1,0:T(8,128)(2,1)} %get-tuple-element.7) | copy-start | bytes 11010052
  119.3 5.2 %copy-start.2 = (bf16[32,8,7296]{2,1,0:T(8,128)(2,1)S(1)}, bf16[32,8,7296]{2,1,0:T(8,128)(2,1)}, u32[]{:S(2)}) copy-start(bf16[32,8,7296]{2,1,0:T(8,128)(2,1)} %get-tuple-element.6) | copy-start | bytes 11206660
  119.3 5.2 %copy-start.3 = (f32[256,512]{1,0:T(8,128)S(1)}, f32[256,512]{1,0:T(8,128)}, u32[]{:S(2)}) copy-start(f32[256,512]{1,0:T(8,128)} %fusion.7) | copy-start | bytes 1572868
  119.3 5.2 %copy-start.4 = (f32[256,512]{1,0:T(8,128)S(1)}, f32[256,512]{1,0:T(8,128)}, u32[]{:S(2)}) copy-start(f32[256,512]{1,0:T(8,128)} %fusion.10) | copy-start | bytes 1572868

commit v4 on v3

--- a/solution.py
+++ b/solution.py
@@ -123,7 +123,7 @@
     slot = lambda d, e, c: g_at(d) * local + z_at(e) * 2 + c
     greet(groups, zs, sibling, by_group, by_z)
     f32 = jnp.float32
-    order = [(d, e) for e in list(range(1, zs)) + [0] for d in list(range(groups - 1, 0, -1)) + [0]]
+    order = [(d, e) for e in list(range(1, zs)) + [0] for d in list(range(1, groups)) + [0]]
 
     def send(src, dst, s_sem, r_sem, peer):
         copy = pltpu.make_async_remote_copy(
@@ -140,36 +140,21 @@
             part.at[slot(d, e, 1 - core)], recv_core.at[k], send1.at[k], got1.at[k], sibling
         )
     second = {}
-    relayed = groups == 4
-
-    def add_and_send(d, e, extra, peer):
+    for d, e in order:
+        if d == 0:
+            continue
         k = d * zs + e
         first[k].wait_recv()
         both = part[slot(d, e, core)].astype(f32) + recv_core[k].astype(f32)
-        if extra:
-            second[3 * zs + e].wait_recv()
-            both = both + recv_group[2 * zs + e].astype(f32)
         sum_core[k - zs] = both.astype(sum_core.dtype)
         second[k] = send(
-            sum_core.at[k - zs], recv_group.at[k - zs], send2.at[k - zs], got2.at[k - zs], by_group(peer)
-        )
-
-    late = list(range(1, zs)) + [0]
-    if relayed:
-        for e in late:
-            add_and_send(3, e, False, 1 + e % 2)
-            add_and_send(1 + e % 2, e, False, 1 + e % 2)
-        for e in late:
-            add_and_send(2 - e % 2, e, True, 2 - e % 2)
-    else:
-        for d, e in order:
-            if d:
-                add_and_send(d, e, False, d)
+            sum_core.at[k - zs], recv_group.at[k - zs], send2.at[k - zs], got2.at[k - zs], by_group(d)
+        )
     third = []
     for e in list(range(1, zs)) + [0]:
         first[e].wait_recv()
         total = part[slot(0, e, core)].astype(f32) + recv_core[e].astype(f32)
-        for d in range(1, 3 if relayed else groups):
+        for d in range(1, groups):
             k = d * zs + e
             second[k].wait_recv()
             total = total + recv_group[k - zs].astype(f32)
@@ -192,6 +177,7 @@
     zs = local // 2
     messages = zs - 1 + zs * (groups - 1) + zs * groups
     anywhere = pl.BlockSpec(memory_space=pl.ANY)
+    landing = pl.BlockSpec(memory_space=pltpu.VMEM)
     return pl.pallas_call(
         functools.partial(gather_kernel, groups, local),
         out_shape=(
@@ -199,13 +185,15 @@
             jax.ShapeDtypeStruct((n,) + g.shape, g.dtype),
         ),
         in_specs=[anywhere] * 2,
-        out_specs=(anywhere, anywhere),
+        out_specs=(landing, landing),
         scratch_shapes=[
             pltpu.SemaphoreType.DMA((2,)),
             pltpu.SemaphoreType.DMA((2, messages)),
             pltpu.SemaphoreType.DMA((2, n)),
         ],
-        compiler_params=pltpu.CompilerParams(collective_id=0, has_side_effects=True),
+        compiler_params=pltpu.CompilerParams(
+            collective_id=0, has_side_effects=True, vmem_limit_bytes=50 * 2**20
+        ),
         name="gather",
     )(x, g)
 

time: 131 us -> 130 us (level)
  matrix products: 43.5 us -> 46.5 us
  Pallas kernels: 79.5 us -> 76.8 us
    pallas_call x1, Pallas kernels: 35.8 us -> 32 us  [reduce(): pl.pallas_call(functools.partial(reduce_kernel, groups, local), out_shape...]
    dot_general x1, matrix products: 5.28 us -> 8.24 us  [body(): part = jnp.dot(d_gate, gate_w.T, preferred_element_type=jnp.float32)]
    dot_general x1, matrix products: 5.62 us -> 7.42 us  [body(): part = part + jnp.dot(d_up, up_w.T, preferred_element_type=jnp.float32)]
where the time goes in v4:
time: 130 us; the launch traced here: 129 us
  Pallas kernels  76.8 us (59%)
  matrix products  46.5 us (36%)
  local copies, waits for them, and re-layouts  4.08 us (3%)
  other arithmetic  1.38 us (1%)
    pallas_call x1, Pallas kernels, gather(): pl.pallas_call(functools.partial(gather_kernel, groups, local), out_shape...  44.7 us
    pallas_call x1, Pallas kernels, reduce(): pl.pallas_call(functools.partial(reduce_kernel, groups, local), out_shape...  32 us
    dot_general x1, matrix products, body(): part = jnp.dot(d_gate, gate_w.T, preferred_element_type=jnp.float32)  8.24 us
    dot_general x1, matrix products, body(): part = part + jnp.dot(d_up, up_w.T, preferred_element_type=jnp.float32)  7.42 us
    dot_general x1, matrix products, body(): pre_gate = jnp.dot(rows_x, gate_w, preferred_element_type=jnp.float32)  6.49 us
    dot_general x1, matrix products, body(): d_hidden = jnp.dot(rows_g, down_w.T, preferred_element_type=jnp.float32)  6.43 us
    dot_general x1, matrix products, body(): jnp.dot(hidden.T, rows_g, preferred_element_type=jnp.float32)  5.34 us
    dot_general x1, matrix products, body(): jnp.dot(rows_x.T, d_gate, preferred_element_type=jnp.float32)  5.32 us

profile of v4, /device:TPU:0, one launch (start us, length us, event | category | flops | bytes accessed | tf_op | source)
XLA Modules:
  0.0 129.5 jit_solution(9101207534292699769)
XLA Ops:
  0.6 0.9 pad.12.x_in
  1.6 0.8 copy.17
  2.3 0.8 copy.16
  3.1 0.1 select_reduce_fusion
  3.2 0.1 fusion.29
  3.3 0.0 slice-start
  3.3 1.1 fusion.21.g_in
  4.4 44.7 %gather.1 = (bf16[32,8,7168]{2,1,0:T(8,128)(2,1)S(1)}, bf16[32,8,7296]{2,1,0:T(8,128)(2,1)}) custom-call(bf16[8,7168]{1,0:T(8,128)(2,1)S(1)} %pad.12.x_in, bf16[8,7296]{1,0:T(8,128)(2,1)S(1)} %fusion.21.g_in), custom_call_target="tpu_custom_call" | custom-call | tf_op jit(solution)/shard_map/gather/pallas_call | solution.py:181
  49.1 0.0 copy-start
  49.1 0.0 slice-start.1
  49.1 6.5 %fusion.7 = f32[256,512]{1,0:T(8,128)S(1)} fusion(bf16[1,7168,512]{2,1,0:T(8,128)(2,1)} %param.11, bf16[32,8,7168]{2,1,0:T(8,128)(2,1)S(1)} %get-tuple-element.7), kind=kOutput, calls=%fused_computation.11 | convolution fusion | flops 1879048192 | bytes 11534336 | tf_op jit(solution)/shard_map/dot_general | solution.py:254
  55.6 0.0 copy-done
  55.6 0.0 slice-done
  55.6 0.0 slice-done.1
  55.7 2.0 %fusion.10 = f32[256,512]{1,0:T(8,128)S(1)} fusion(bf16[1,7168,512]{2,1,0:T(8,128)(2,1)S(1)} %bitcast.44, bf16[32,8,7168]{2,1,0:T(8,128)(2,1)S(1)} %get-tuple-element.7), kind=kOutput, calls=%fused_computation.14 | convolution fusion | flops 1879048192 | bytes 11534336 | tf_op jit(solution)/shard_map/dot_general | solution.py:255
  57.7 0.8 slice.24
  58.6 0.1 copy.19
  58.7 0.1 fusion.23
  58.8 6.4 %multiply_convert_fusion.4 = (bf16[256,512]{1,0:T(8,128)(2,1)S(1)}, bf16[256,512]{1,0:T(8,128)(2,1)S(1)}) fusion(f32[256,512]{1,0:T(8,128)S(1)} %fusion.7, f32[256,512]{1,0:T(8,128)S(1)} %fusion.10, bf16[1,512,7168]{2,1,0:T(8,128)(2,1)} %param.13, bf16[256,7296]{1,0:T(8,128)(2,1)} %bitcast.46, f32[256]{0:T(256)S(1)} %bitcast.48), kind=kOutput, calls=%fused_computation.24 | convolution fusion | flops 1886257152 | bytes 12583936 | tf_op jit(solution)/shard_map/dot_general | solution.py:258
  65.2 8.2 %fusion.5 = f32[256,7168]{1,0:T(8,128)} fusion(bf16[256,512]{1,0:T(8,128)(2,1)S(1)} %get-tuple-element.9, bf16[1,7168,512]{2,1,0:T(8,128)(2,1)} %param.11), kind=kOutput, calls=%fused_computation.9 | convolution fusion | flops 1879048192 | bytes 14942208 | tf_op jit(solution)/shard_map/dot_general | solution.py:261
  73.4 0.0 copy-start.1
  73.4 7.4 %fusion.4.part = bf16[32,8,7168]{2,1,0:T(8,128)(2,1)S(1)} fusion(f32[256,7168]{1,0:T(8,128)} %fusion.5, bf16[256,512]{1,0:T(8,128)(2,1)S(1)} %get-tuple-element.8, bf16[1,7168,512]{2,1,0:T(8,128)(2,1)} %param.12), kind=kOutput, calls=%fused_computation.8 | convolution fusion | flops 1882718208 | bytes 18612224 | tf_op jit(solution)/shard_map/dot_general | solution.py:262
  80.9 32.0 %reduce.1 = f32[8,7168]{1,0:T(8,128)S(1)} custom-call(bf16[32,8,7168]{2,1,0:T(8,128)(2,1)S(1)} %fusion.4.part), custom_call_target="tpu_custom_call" | custom-call | tf_op jit(solution)/shard_map/reduce/pallas_call | solution.py:207
  112.9 0.0 copy-done.1
  112.9 5.3 %fusion = bf16[1,7168,512]{2,1,0:T(8,128)(2,1)} fusion(bf16[256,512]{1,0:T(8,128)(2,1)S(1)} %get-tuple-element.9, bf16[32,8,7168]{2,1,0:T(8,128)(2,1)S(1)} %copy-done.1), kind=kOutput, calls=%fused_computation.3 | convolution fusion | flops 1882718208 | bytes 11272192 | tf_op jit(solution)/shard_map/dot_general | solution.py:266
  118.3 0.0 copy-start.2
  118.3 5.2 %fusion.1 = bf16[1,7168,512]{2,1,0:T(8,128)(2,1)} fusion(bf16[256,512]{1,0:T(8,128)(2,1)S(1)} %get-tuple-element.8, bf16[32,8,7168]{2,1,0:T(8,128)(2,1)S(1)} %copy-done.1), kind=kOutput, calls=%fused_computation.4 | convolution fusion | flops 1882718208 | bytes 11272192 | tf_op jit(solution)/shard_map/dot_general | solution.py:267
  123.4 0.0 copy-done.2
  123.4 5.3 %fusion.2 = bf16[1,512,7168]{2,1,0:T(8,128)(2,1)} fusion(bf16[256,7296]{1,0:T(8,128)(2,1)S(1)} %bitcast.47, f32[256]{0:T(256)S(1)} %bitcast.49, f32[256,512]{1,0:T(8,128)S(1)} %fusion.10, f32[256,512]{1,0:T(8,128)S(1)} %fusion.7), kind=kOutput, calls=%fused_computation.5 | convolution fusion | flops 1889009664 | bytes 12059648 | tf_op jit(solution)/shard_map/dot_general | solution.py:265
  128.8 0.7 copy.21
  (4 shorter events, 0.0 us)
Async XLA Ops:
  3.3 52.4 %slice-start = ((s8[7340032]{0:T(1024)(128)(4,1)}), s8[3145728]{0:T(1024)(128)(4,1)S(1)}, s32[]{:S(2)}) async-start(s8[7340032]{0:T(1024)(128)(4,1)} %bitcast.43), calls=%async_computation | async-start | bytes 6291456
  49.1 6.5 %copy-start = (bf16[32,8,7168]{2,1,0:T(8,128)(2,1)}, bf16[32,8,7168]{2,1,0:T(8,128)(2,1)S(1)}, u32[]{:S(2)}) copy-start(bf16[32,8,7168]{2,1,0:T(8,128)(2,1)S(1)} %get-tuple-element.7) | copy-start | bytes 11010052
  49.1 6.5 %slice-start.1 = ((s8[7340032]{0:T(1024)(128)(4,1)}), s8[4194304]{0:T(1024)(128)(4,1)S(1)}, s32[]{:S(2)}) async-start(s8[7340032]{0:T(1024)(128)(4,1)} %bitcast.43), calls=%async_computation.1 | async-start | bytes 8388608
  73.4 39.5 %copy-start.1 = (bf16[32,8,7168]{2,1,0:T(8,128)(2,1)S(1)}, bf16[32,8,7168]{2,1,0:T(8,128)(2,1)}, u32[]{:S(2)}) copy-start(bf16[32,8,7168]{2,1,0:T(8,128)(2,1)} %copy-done) | copy-start | bytes 11010052
  118.3 5.2 %copy-start.2 = (bf16[32,8,7296]{2,1,0:T(8,128)(2,1)S(1)}, bf16[32,8,7296]{2,1,0:T(8,128)(2,1)}, u32[]{:S(2)}) copy-start(bf16[32,8,7296]{2,1,0:T(8,128)(2,1)} %get-tuple-element.6) | copy-start | bytes 11206660

commit v5 on v4

--- a/solution.py
+++ b/solution.py
@@ -177,7 +177,6 @@
     zs = local // 2
     messages = zs - 1 + zs * (groups - 1) + zs * groups
     anywhere = pl.BlockSpec(memory_space=pl.ANY)
-    landing = pl.BlockSpec(memory_space=pltpu.VMEM)
     return pl.pallas_call(
         functools.partial(gather_kernel, groups, local),
         out_shape=(
@@ -185,15 +184,13 @@
             jax.ShapeDtypeStruct((n,) + g.shape, g.dtype),
         ),
         in_specs=[anywhere] * 2,
-        out_specs=(landing, landing),
+        out_specs=(anywhere, anywhere),
         scratch_shapes=[
             pltpu.SemaphoreType.DMA((2,)),
             pltpu.SemaphoreType.DMA((2, messages)),
             pltpu.SemaphoreType.DMA((2, n)),
         ],
-        compiler_params=pltpu.CompilerParams(
-            collective_id=0, has_side_effects=True, vmem_limit_bytes=50 * 2**20
-        ),
+        compiler_params=pltpu.CompilerParams(collective_id=0, has_side_effects=True),
         name="gather",
     )(x, g)
 

time: 130 us -> 127 us (0.977)
  matrix products: 46.5 us -> 43.5 us
    dot_general x1, matrix products: 8.24 us -> 5.28 us  [body(): part = jnp.dot(d_gate, gate_w.T, preferred_element_type=jnp.float32)]
    dot_general x1, matrix products: 7.42 us -> 5.62 us  [body(): part = part + jnp.dot(d_up, up_w.T, preferred_element_type=jnp.float32)]
where the time goes in v5:
time: 127 us
  Pallas kernels  75.7 us (60%)
  matrix products  43.5 us (34%)
  local copies, waits for them, and re-layouts  4.73 us (4%)
  other arithmetic  2.02 us (2%)
    pallas_call x1, Pallas kernels, gather(): pl.pallas_call(functools.partial(gather_kernel, groups, local), out_shape...  43.7 us
    pallas_call x1, Pallas kernels, reduce(): pl.pallas_call(functools.partial(reduce_kernel, groups, local), out_shape...  32 us
    dot_general x1, matrix products, body(): pre_gate = jnp.dot(rows_x, gate_w, preferred_element_type=jnp.float32)  7.19 us
    dot_general x1, matrix products, body(): d_hidden = jnp.dot(rows_g, down_w.T, preferred_element_type=jnp.float32)  6.56 us
    dot_general x1, matrix products, body(): part = part + jnp.dot(d_up, up_w.T, preferred_element_type=jnp.float32)  5.62 us
    dot_general x1, matrix products, body(): jnp.dot(rows_x.T, d_gate, preferred_element_type=jnp.float32)  5.37 us
    dot_general x1, matrix products, body(): jnp.dot(hidden.T, rows_g, preferred_element_type=jnp.float32)  5.34 us
    dot_general x1, matrix products, body(): part = jnp.dot(d_gate, gate_w.T, preferred_element_type=jnp.float32)  5.28 us

profile of v5, /device:TPU:0, one launch (start us, length us, event | category | flops | bytes accessed | tf_op | source)
XLA Modules:
  0.0 126.7 jit_solution(12950802571897884434)
XLA Ops:
  0.6 1.6 %pad.12.x_in = bf16[8,7168]{1,0:T(8,128)(2,1)} pad(bf16[6,7168]{1,0:T(8,128)(2,1)} %param.7, bf16[]{:T(256)} %constant.2.clone.1), padding=0_2x0_0 | pad | bytes 200706 | tf_op jit(solution)/shard_map/jit(_pad)/pad | solution.py:238
  2.2 0.8 copy.17
  3.0 0.8 copy.16
  3.7 0.1 select_reduce_fusion
  3.8 0.1 fusion.29
  3.9 0.0 slice-start
  3.9 1.7 %fusion.21.g_in = bf16[8,7296]{1,0:T(8,128)(2,1)} fusion(bf16[6,128]{1,0:T(8,128)(2,1)S(1)} %fusion.29, bf16[6,7168]{1,0:T(8,128)(2,1)} %param.8), kind=kLoop, calls=%fused_computation.31 | loop fusion | flops 408576 | bytes 204288 | tf_op jit(solution)/shard_map/concatenate | solution.py:239
  5.7 43.7 %gather.1 = (bf16[32,8,7168]{2,1,0:T(8,128)(2,1)}, bf16[32,8,7296]{2,1,0:T(8,128)(2,1)}) custom-call(bf16[8,7168]{1,0:T(8,128)(2,1)} %pad.12.x_in, bf16[8,7296]{1,0:T(8,128)(2,1)} %fusion.21.g_in), custom_call_target="tpu_custom_call" | custom-call | tf_op jit(solution)/shard_map/gather/pallas_call | solution.py:180
  49.4 0.0 copy-start
  49.4 0.0 slice-start.1
  49.4 7.2 %fusion.7 = f32[256,512]{1,0:T(8,128)} fusion(bf16[1,7168,512]{2,1,0:T(8,128)(2,1)} %param.11, bf16[32,8,7168]{2,1,0:T(8,128)(2,1)} %get-tuple-element.7), kind=kOutput, calls=%fused_computation.11 | convolution fusion | flops 1879048192 | bytes 11534336 | tf_op jit(solution)/shard_map/dot_general | solution.py:251
  56.6 0.0 slice-done
  56.6 0.0 copy-done
  56.6 0.0 slice-done.1
  56.6 3.0 %fusion.10 = f32[256,512]{1,0:T(8,128)} fusion(bf16[1,7168,512]{2,1,0:T(8,128)(2,1)S(1)} %bitcast.44, bf16[32,8,7168]{2,1,0:T(8,128)(2,1)S(1)} %copy-done), kind=kOutput, calls=%fused_computation.14 | convolution fusion | flops 1879048192 | bytes 11534336 | tf_op jit(solution)/shard_map/dot_general | solution.py:252
  59.6 0.8 slice.24
  60.4 0.1 copy.19
  60.5 0.1 fusion.23
  60.6 6.6 %multiply_convert_fusion.4 = (bf16[256,512]{1,0:T(8,128)(2,1)S(1)}, bf16[256,512]{1,0:T(8,128)(2,1)S(1)}) fusion(f32[256,512]{1,0:T(8,128)} %fusion.7, f32[256,512]{1,0:T(8,128)} %fusion.10, bf16[1,512,7168]{2,1,0:T(8,128)(2,1)} %param.13, bf16[256,7296]{1,0:T(8,128)(2,1)} %bitcast.46, f32[256]{0:T(256)S(1)} %bitcast.48), kind=kOutput, calls=%fused_computation.24 | convolution fusion | flops 1886257152 | bytes 12583936 | tf_op jit(solution)/shard_map/dot_general | solution.py:255
  67.2 5.3 %fusion.5 = f32[256,7168]{1,0:T(8,128)S(1)} fusion(bf16[256,512]{1,0:T(8,128)(2,1)S(1)} %get-tuple-element.9, bf16[1,7168,512]{2,1,0:T(8,128)(2,1)} %param.11), kind=kOutput, calls=%fused_computation.9 | convolution fusion | flops 1879048192 | bytes 14942208 | tf_op jit(solution)/shard_map/dot_general | solution.py:258
  72.5 0.0 copy-start.1
  72.5 5.6 %fusion.4.part = bf16[32,8,7168]{2,1,0:T(8,128)(2,1)S(1)} fusion(f32[256,7168]{1,0:T(8,128)S(1)} %fusion.5, bf16[256,512]{1,0:T(8,128)(2,1)S(1)} %get-tuple-element.8, bf16[1,7168,512]{2,1,0:T(8,128)(2,1)} %param.12), kind=kOutput, calls=%fused_computation.8 | convolution fusion | flops 1882718208 | bytes 18612224 | tf_op jit(solution)/shard_map/dot_general | solution.py:259
  78.1 32.0 %reduce.1 = f32[8,7168]{1,0:T(8,128)S(1)} custom-call(bf16[32,8,7168]{2,1,0:T(8,128)(2,1)S(1)} %fusion.4.part), custom_call_target="tpu_custom_call" | custom-call | tf_op jit(solution)/shard_map/reduce/pallas_call | solution.py:204
  110.1 0.0 copy-done.1
  110.1 5.4 %fusion = bf16[1,7168,512]{2,1,0:T(8,128)(2,1)} fusion(bf16[256,512]{1,0:T(8,128)(2,1)S(1)} %get-tuple-element.9, bf16[32,8,7168]{2,1,0:T(8,128)(2,1)S(1)} %copy-done.1), kind=kOutput, calls=%fused_computation.3 | convolution fusion | flops 1882718208 | bytes 11272192 | tf_op jit(solution)/shard_map/dot_general | solution.py:263
  115.5 0.0 copy-start.2
  115.5 0.0 copy-start.3
  115.5 0.0 copy-start.4
  115.5 5.2 %fusion.1 = bf16[1,7168,512]{2,1,0:T(8,128)(2,1)} fusion(bf16[256,512]{1,0:T(8,128)(2,1)S(1)} %get-tuple-element.8, bf16[32,8,7168]{2,1,0:T(8,128)(2,1)S(1)} %copy-done.1), kind=kOutput, calls=%fused_computation.4 | convolution fusion | flops 1882718208 | bytes 11272192 | tf_op jit(solution)/shard_map/dot_general | solution.py:264
  120.7 0.0 copy-done.2
  120.7 0.0 copy-done.3
  120.7 0.0 copy-done.4
  120.7 5.3 %fusion.2 = bf16[1,512,7168]{2,1,0:T(8,128)(2,1)} fusion(bf16[256,7296]{1,0:T(8,128)(2,1)S(1)} %bitcast.47, f32[256]{0:T(256)S(1)} %bitcast.49, f32[256,512]{1,0:T(8,128)S(1)} %copy-done.4, f32[256,512]{1,0:T(8,128)S(1)} %copy-done.3), kind=kOutput, calls=%fused_computation.5 | convolution fusion | flops 1889009664 | bytes 12059648 | tf_op jit(solution)/shard_map/dot_general | solution.py:262
  126.0 0.7 copy.21
  (4 shorter events, 0.0 us)
Async XLA Ops:
  3.9 52.7 %slice-start = ((s8[7340032]{0:T(1024)(128)(4,1)}), s8[3145728]{0:T(1024)(128)(4,1)S(1)}, s32[]{:S(2)}) async-start(s8[7340032]{0:T(1024)(128)(4,1)} %bitcast.43), calls=%async_computation | async-start | bytes 6291456
  49.4 7.2 %copy-start = (bf16[32,8,7168]{2,1,0:T(8,128)(2,1)S(1)}, bf16[32,8,7168]{2,1,0:T(8,128)(2,1)}, u32[]{:S(2)}) copy-start(bf16[32,8,7168]{2,1,0:T(8,128)(2,1)} %get-tuple-element.7) | copy-start | bytes 11010052
  49.4 7.2 %slice-start.1 = ((s8[7340032]{0:T(1024)(128)(4,1)}), s8[4194304]{0:T(1024)(128)(4,1)S(1)}, s32[]{:S(2)}) async-start(s8[7340032]{0:T(1024)(128)(4,1)} %bitcast.43), calls=%async_computation.1 | async-start | bytes 8388608
  72.5 37.6 %copy-start.1 = (bf16[32,8,7168]{2,1,0:T(8,128)(2,1)S(1)}, bf16[32,8,7168]{2,1,0:T(8,128)(2,1)}, u32[]{:S(2)}) copy-start(bf16[32,8,7168]{2,1,0:T(8,128)(2,1)} %get-tuple-element.7) | copy-start | bytes 11010052
  115.5 5.2 %copy-start.2 = (bf16[32,8,7296]{2,1,0:T(8,128)(2,1)S(1)}, bf16[32,8,7296]{2,1,0:T(8,128)(2,1)}, u32[]{:S(2)}) copy-start(bf16[32,8,7296]{2,1,0:T(8,128)(2,1)} %get-tuple-element.6) | copy-start | bytes 11206660
  115.5 5.2 %copy-start.3 = (f32[256,512]{1,0:T(8,128)S(1)}, f32[256,512]{1,0:T(8,128)}, u32[]{:S(2)}) copy-start(f32[256,512]{1,0:T(8,128)} %fusion.7) | copy-start | bytes 1572868
  115.5 5.2 %copy-start.4 = (f32[256,512]{1,0:T(8,128)S(1)}, f32[256,512]{1,0:T(8,128)}, u32[]{:S(2)}) copy-start(f32[256,512]{1,0:T(8,128)} %fusion.10) | copy-start | bytes 1572868
